TPU v7x, 32 devices: a whole 2x2x4 slice. The times are simulated.
32 devices in a mesh: dp: 4 (over z), row: 4 (over x, core), col: 2 (over y).
Axes of the slice: x: 2, y: 2, z: 4, core: 2. Of those that a mesh axis runs over, the one named last changes fastest.
Arguments:
- tokens: bfloat16 [8192, 2048], P(('dp', 'row'), 'col'), may hold values from -6 to 6
- grad_out: bfloat16 [8192, 2048], P(('dp', 'row'), 'col'), may hold values from -6 to 6
- first_gain: float32 [2048], P('col'), may hold values from 0.1 to 1.9
- query_weight: bfloat16 [2048, 2048], P('col', 'row'), may hold values from -0.125 to 0.125
- key_weight: bfloat16 [2048, 2048], P('col', 'row'), may hold values from -0.125 to 0.125
- value_weight: bfloat16 [2048, 4096], P('col', 'row'), may hold values from -0.125 to 0.125
- swish_weight: bfloat16 [2048, 4096], P('col', 'row'), may hold values from -0.125 to 0.125
- group_gain: float32 [4096], P(('row', 'col')), may hold values from 0.1 to 1.9
- output_weight: bfloat16 [4096, 2048], P('row', 'col'), may hold values from -0.1875 to 0.1875
- second_gain: float32 [2048], P('col'), may hold values from 0.1 to 1.9
- gate_weight: bfloat16 [2048, 4096], P('col', 'row'), may hold values from -0.125 to 0.125
- up_weight: bfloat16 [2048, 4096], P('col', 'row'), may hold values from -0.125 to 0.125
- down_weight: bfloat16 [4096, 2048], P('row', 'col'), may hold values from -0.125 to 0.125
- decay_rate: float32 [8], P(('row', 'col')), may hold values from 0.00012207031 to 0.03515625
Outputs:
- block_out: bfloat16 [8192, 2048], P(('dp', 'row'), 'col')
- input_grad: float32 [8192, 2048], P(('dp', 'row'), 'col')
- first_gain_grad: float32 [2048], P('col')
- query_grad: float32 [2048, 2048], P('col', 'row')
- key_grad: float32 [2048, 2048], P('col', 'row')
- value_grad: float32 [2048, 4096], P('col', 'row')
- swish_grad: float32 [2048, 4096], P('col', 'row')
- group_gain_grad: float32 [4096], P(('row', 'col'))
- output_grad: float32 [4096, 2048], P('row', 'col')
- second_gain_grad: float32 [2048], P('col')
- gate_grad: float32 [2048, 4096], P('col', 'row')
- up_grad: float32 [2048, 4096], P('col', 'row')
- down_grad: float32 [4096, 2048], P('row', 'col')
All inputs are finite; a program needn't handle non-finite values.
Results may differ from a plain program's by a relative error of at most 0.01405.
Values may be sent and summed in bfloat16 or wider, within the bound.
No kernel may reach another device: no remote copies, remote signals or barrier semaphores. Data moves between devices by JAX's collectives and lax.ppermute only.
A program may use at most 256 MiB of HBM per device.

v0:
```python
import jax
import jax.numpy as jnp
from jax import lax
from jax.sharding import PartitionSpec as P

LEN = 1024


EPS = 1e-05
ROTARY_BASE = 10000.0


def token_gather(row_block):
    return lax.all_gather(row_block, "row", axis=0, tiled=True)


def row_total(term_fn, row_count):
    return lax.psum_scatter(
        term_fn(jnp.int32(0), row_count * lax.axis_size("row")),
        "row",
        scatter_dimension=0,
        tiled=True,
    )


def share_gather(row_block):
    return lax.all_gather(row_block, "col", axis=0, tiled=True)


def share_total(row_block):
    return lax.psum_scatter(row_block, "col", scatter_dimension=0, tiled=True)


def width_total(column):
    return lax.psum(column, "col")


def contract_rows(left, right):
    return lax.dot_general(
        left, right, (((0,), (0,)), ((), ())), preferred_element_type=jnp.float32
    )


def contract_cols(left, right):
    return lax.dot_general(
        left, right, (((1,), (1,)), ((), ())), preferred_element_type=jnp.float32
    )


def layer_normalize(row_block, gain_row):
    full_width = row_block.shape[1] * lax.axis_size("col")
    average = width_total(jnp.sum(row_block, 1, keepdims=True)) / full_width
    centred = row_block - average
    variance = width_total(jnp.sum(centred * centred, 1, keepdims=True)) / full_width
    inverse_deviation = lax.rsqrt(variance + EPS)
    normed = centred * inverse_deviation
    return (normed, inverse_deviation, (normed * gain_row).astype(jnp.bfloat16))


def norm_back(grad_rows, normed, inverse_deviation, gain_row):
    full_width = grad_rows.shape[1] * lax.axis_size("col")
    scaled = grad_rows * gain_row
    first_sum = jnp.sum(scaled, 1, keepdims=True)
    second_sum = jnp.sum(scaled * normed, 1, keepdims=True)
    first_sum = width_total(first_sum)
    second_sum = width_total(second_sum)
    grad_in = inverse_deviation * (
        scaled - first_sum / full_width - normed * (second_sum / full_width)
    )
    return (grad_in, jnp.sum(grad_rows * normed, 0))


def rotate(values, cosine, sine_part):
    half_width = values.shape[1] // 2
    front_part = values[:, :half_width]
    back_part = values[:, half_width:]
    return jnp.concatenate(
        (front_part * cosine - back_part * sine_part, front_part * sine_part + back_part * cosine),
        1,
    )


def rotate_back(gradient, cosine, sine_part):
    half_width = gradient.shape[1] // 2
    front_part = gradient[:, :half_width]
    back_part = gradient[:, half_width:]
    return jnp.concatenate(
        (front_part * cosine + back_part * sine_part, back_part * cosine - front_part * sine_part),
        1,
    )


def make_decay(length, head_rate):
    step_ids = jnp.arange(length, dtype=jnp.int32)
    distance = step_ids[:, None] - step_ids[None, :]
    return jnp.where(
        distance >= 0, jnp.exp(-head_rate * jnp.maximum(distance, 0).astype(jnp.float32)), 0.0
    )


def body(
    tokens,
    grad_out,
    first_gain,
    query_weight,
    key_weight,
    value_weight,
    swish_weight,
    group_gain,
    output_weight,
    second_gain,
    gate_weight,
    up_weight,
    down_weight,
    decay_rate,
):
    row_count = tokens.shape[0]
    tokens_rep = row_count * lax.axis_size("row")
    sequences = tokens_rep // LEN
    input_rows = tokens.astype(jnp.float32)
    first_normed, first_inv, first_in = layer_normalize(input_rows, first_gain)
    first_full = token_gather(first_in)
    queries, keys_pre, valued, swish_in = (
        lax.psum_scatter(
            jnp.dot(first_full, query_weight, preferred_element_type=jnp.float32),
            "col",
            scatter_dimension=1,
            tiled=True,
        ),
        lax.psum_scatter(
            jnp.dot(first_full, key_weight, preferred_element_type=jnp.float32),
            "col",
            scatter_dimension=1,
            tiled=True,
        ),
        lax.psum_scatter(
            jnp.dot(first_full, value_weight, preferred_element_type=jnp.float32),
            "col",
            scatter_dimension=1,
            tiled=True,
        ),
        lax.psum_scatter(
            jnp.dot(first_full, swish_weight, preferred_element_type=jnp.float32),
            "col",
            scatter_dimension=1,
            tiled=True,
        ),
    )
    positions = (jnp.arange(tokens_rep, dtype=jnp.int32) % LEN).astype(jnp.float32)
    half_width = queries.shape[1] // 2
    frequency = ROTARY_BASE ** (-jnp.arange(half_width, dtype=jnp.float32) / half_width)
    rotation = positions[:, None] * frequency[None, :]
    cosine = jnp.cos(rotation)
    sine_part = jnp.sin(rotation)
    query_rot = rotate(queries, cosine, sine_part).astype(jnp.bfloat16)
    key_rot = rotate(keys_pre, cosine, sine_part).astype(jnp.bfloat16)
    value_low = valued.astype(jnp.bfloat16)
    decay_mask = make_decay(LEN, decay_rate[0])
    key_size = query_rot.shape[1]
    value_size = value_low.shape[1]

    def retention_apply(segment):
        query_sequence_rows, key_sequence_rows, value_seq = segment
        score_matrix = jnp.einsum(
            "nd,md->nm", query_sequence_rows, key_sequence_rows, preferred_element_type=jnp.float32
        )
        weighted = (score_matrix * decay_mask).astype(jnp.bfloat16)
        return jnp.dot(weighted, value_seq, preferred_element_type=jnp.float32)

    retained = lax.map(
        retention_apply,
        (
            query_rot.reshape(sequences, LEN, key_size),
            key_rot.reshape(sequences, LEN, key_size),
            value_low.reshape(sequences, LEN, value_size),
        ),
    ).reshape(tokens_rep, value_size)
    average = jnp.mean(retained, 1, keepdims=True)
    centred = retained - average
    variance = jnp.mean(centred * centred, 1, keepdims=True)
    floor_open = (variance > 1.0).astype(jnp.float32)
    group_inv = lax.rsqrt(jnp.maximum(variance, 1.0))
    normed_o = centred * group_inv
    swish_out, swish_pull = jax.vjp(jax.nn.silu, swish_in)
    gated = (swish_out * normed_o * group_gain).astype(jnp.bfloat16)
    paired = lax.all_gather(gated, "col", axis=1, tiled=True)

    def project_out(first_row, span):
        return jnp.dot(paired, output_weight, preferred_element_type=jnp.float32)

    x_mid = input_rows + row_total(project_out, row_count)
    second_normed, second_inv, second_in = layer_normalize(x_mid, second_gain)
    second_full = token_gather(second_in)
    gate_up_weight = jnp.concatenate((gate_weight, up_weight), 1)
    hidden_dev = gate_weight.shape[1]
    gate_up = share_total(jnp.dot(second_full, gate_up_weight, preferred_element_type=jnp.float32))
    gate_pre = gate_up[:, :hidden_dev]
    up_pre = gate_up[:, hidden_dev:]
    gelu_val, gelu_pull = jax.vjp(jax.nn.gelu, gate_pre)
    hidden = (gelu_val * up_pre).astype(jnp.bfloat16)
    hidden_full = share_gather(hidden)

    def project_down(first_row, span):
        return jnp.dot(hidden_full, down_weight, preferred_element_type=jnp.float32)

    block_out = (x_mid + row_total(project_down, row_count)).astype(jnp.bfloat16)
    down_in = token_gather(grad_out)
    down_grad = contract_rows(hidden_full, down_in)
    grad_hidden = share_total(contract_cols(down_in, down_weight))
    grad_gate = gelu_pull(grad_hidden * up_pre)[0]
    grad_up = grad_hidden * gelu_val
    grad_both = share_gather(jnp.concatenate((grad_gate, grad_up), 1).astype(jnp.bfloat16))
    gate_up_grad = contract_rows(second_full, grad_both)
    gate_grad = gate_up_grad[:, :hidden_dev]
    up_grad = gate_up_grad[:, hidden_dev:]

    def back_mlp(first_row, span):
        return contract_cols(grad_both, gate_up_weight)

    grad_second = row_total(back_mlp, row_count)
    grad_norm_mid, second_gain_part = norm_back(grad_second, second_normed, second_inv, second_gain)
    grad_mid = grad_out.astype(jnp.float32) + grad_norm_mid
    attn_in = token_gather(grad_mid.astype(jnp.bfloat16))
    output_grad = contract_rows(paired, attn_in)
    grad_gated = lax.psum_scatter(
        contract_cols(attn_in, output_weight), "col", scatter_dimension=1, tiled=True
    )
    group_gain_part = jnp.sum(grad_gated * swish_out * normed_o, 0)
    grad_product = grad_gated * group_gain
    grad_normed_o = grad_product * swish_out
    grad_swish = swish_pull(grad_product * normed_o)[0].astype(jnp.bfloat16)
    grad_retained = (
        group_inv
        * (
            grad_normed_o
            - jnp.mean(grad_normed_o, 1, keepdims=True)
            - floor_open * normed_o * jnp.mean(grad_normed_o * normed_o, 1, keepdims=True)
        )
    ).astype(jnp.bfloat16)

    def retain_back(segment):
        query_sequence_rows, key_sequence_rows, value_seq, grad_seq = segment
        score_matrix = jnp.einsum(
            "nd,md->nm", query_sequence_rows, key_sequence_rows, preferred_element_type=jnp.float32
        )
        weighted = (score_matrix * decay_mask).astype(jnp.bfloat16)
        value_gradient_rows = jnp.einsum(
            "nm,ne->me", weighted, grad_seq, preferred_element_type=jnp.float32
        )
        grad_scores = (
            jnp.einsum("ne,me->nm", grad_seq, value_seq, preferred_element_type=jnp.float32)
            * decay_mask
        ).astype(jnp.bfloat16)
        grad_query_seq = jnp.dot(grad_scores, key_sequence_rows, preferred_element_type=jnp.float32)
        grad_key_seq = jnp.einsum(
            "nm,nd->md", grad_scores, query_sequence_rows, preferred_element_type=jnp.float32
        )
        return (grad_query_seq, grad_key_seq, value_gradient_rows.astype(jnp.bfloat16))

    grad_qrot, grad_krot, grad_valued = lax.map(
        retain_back,
        (
            query_rot.reshape(sequences, LEN, key_size),
            key_rot.reshape(sequences, LEN, key_size),
            value_low.reshape(sequences, LEN, value_size),
            grad_retained.reshape(sequences, LEN, value_size),
        ),
    )
    grad_queries = rotate_back(grad_qrot.reshape(tokens_rep, key_size), cosine, sine_part).astype(
        jnp.bfloat16
    )
    grad_keys = rotate_back(grad_krot.reshape(tokens_rep, key_size), cosine, sine_part).astype(
        jnp.bfloat16
    )
    grad_valued = grad_valued.reshape(tokens_rep, value_size)
    query_pair, key_pair, value_pair, swish_pair = (
        lax.all_gather(grad_queries, "col", axis=1, tiled=True),
        lax.all_gather(grad_keys, "col", axis=1, tiled=True),
        lax.all_gather(grad_valued, "col", axis=1, tiled=True),
        lax.all_gather(grad_swish, "col", axis=1, tiled=True),
    )
    query_grad = contract_rows(first_full, query_pair)
    key_grad = contract_rows(first_full, key_pair)
    value_grad = contract_rows(first_full, value_pair)
    swish_grad = contract_rows(first_full, swish_pair)

    def back_heads(first_row, span):
        total = contract_cols(query_pair, query_weight)
        total = total + contract_cols(key_pair, key_weight)
        total = total + contract_cols(value_pair, value_weight)
        return total + contract_cols(swish_pair, swish_weight)

    grad_first = row_total(back_heads, row_count)
    grad_norm_in, first_gain_part = norm_back(grad_first, first_normed, first_inv, first_gain)
    input_grad = grad_mid + grad_norm_in
    first_gain_grad, second_gain_grad = lax.psum((first_gain_part, second_gain_part), ("dp", "row"))
    (
        query_grad,
        key_grad,
        value_grad,
        swish_grad,
        group_gain_grad,
        output_grad,
        gate_grad,
        up_grad,
        down_grad,
    ) = lax.psum(
        (
            query_grad,
            key_grad,
            value_grad,
            swish_grad,
            group_gain_part,
            output_grad,
            gate_grad,
            up_grad,
            down_grad,
        ),
        "dp",
    )
    return (
        block_out,
        input_grad,
        first_gain_grad,
        query_grad,
        key_grad,
        value_grad,
        swish_grad,
        group_gain_grad,
        output_grad,
        second_gain_grad,
        gate_grad,
        up_grad,
        down_grad,
    )


def solution(mesh):
    placed = (
        P(("dp", "row"), "col"),
        P(("dp", "row"), "col"),
        P("col"),
        P("col", "row"),
        P("col", "row"),
        P("col", "row"),
        P("col", "row"),
        P(("row", "col")),
        P("row", "col"),
        P("col"),
        P("col", "row"),
        P("col", "row"),
        P("row", "col"),
        P(("row", "col")),
    )
    return jax.shard_map(
        body,
        mesh=mesh,
        in_specs=placed,
        out_specs=(
            P(("dp", "row"), "col"),
            P(("dp", "row"), "col"),
            P("col"),
            P("col", "row"),
            P("col", "row"),
            P("col", "row"),
            P("col", "row"),
            P(("row", "col")),
            P("row", "col"),
            P("col"),
            P("col", "row"),
            P("col", "row"),
            P("row", "col"),
        ),
        check_vma=False,
    )
```

profile of v0, /device:TPU:0, one launch (start us, length us, event | category | flops | bytes accessed | tf_op | source)
XLA Modules:
  0.0 2693.5 jit_solution(18372181613220177278)
XLA Ops:
  24.6 36.4 %all-gather.12.cloned.1.call-done = bf16[2048,1024]{1,0:T(8,128)(2,1)} async-done(((bf16[512,1024]{1,0:T(8,128)(2,1)}), bf16[2048,1024]{1,0:T(8,128)(2,1)}) %all-gather.12.cloned.1.call-update) | async-done | bytes 4194320 | tf_op jit(solution)/shard_map/all_gather | solution.py:14
  97.9 24.1 reduce-scatter.16.cloned.1.call-done
  122.0 57.3 %reduce-scatter.14.cloned.1.call-done = f32[2048,256]{1,0:T(8,128)} async-done(((f32[2048,512]{1,0:T(8,128)}), f32[2048,256]{1,0:T(8,128)}) %reduce-scatter.14.cloned.1.call-update) | async-done | bytes 2097168 | tf_op jit(solution)/shard_map/reduce_scatter | solution.py:124
  188.0 92.8 %reduce-scatter.18.cloned.1.call-done = f32[2048,512]{1,0:T(8,128)} async-done(((f32[2048,1024]{1,0:T(8,128)}), f32[2048,512]{1,0:T(8,128)}) %reduce-scatter.18.cloned.1.call-update) | async-done | bytes 4194320 | tf_op jit(solution)/shard_map/reduce_scatter | solution.py:136
  300.0 82.3 %reduce-scatter.12.cloned.1.call-done = f32[2048,512]{1,0:T(8,128)} async-done(((f32[2048,1024]{1,0:T(8,128)}), f32[2048,512]{1,0:T(8,128)}) %reduce-scatter.12.cloned.1.call-update) | async-done | bytes 4194320 | tf_op jit(solution)/shard_map/reduce_scatter | solution.py:142
  387.9 56.4 %all-gather.14.cloned.1.call-done = bf16[2048,1024]{1,0:T(8,128)(2,1)} async-done(((bf16[2048,512]{1,0:T(8,128)(2,1)}), bf16[2048,1024]{1,0:T(8,128)(2,1)}) %all-gather.14.cloned.1.call-update) | async-done | bytes 4194320 | tf_op jit(solution)/shard_map/all_gather | solution.py:186
  455.9 71.1 %reduce-scatter.20.cloned.1.call-done = f32[512,1024]{1,0:T(8,128)} async-done(((f32[2048,1024]{1,0:T(8,128)}), f32[512,1024]{1,0:T(8,128)}) %reduce-scatter.20.cloned.1.call-update) | async-done | bytes 2097168 | tf_op jit(solution)/shard_map/reduce_scatter | solution.py:18
  545.1 18.0 all-gather.20.cloned.1.call-done
  577.3 22.6 all-gather.16.cloned.1.call-done
  615.0 86.3 %reduce-scatter.26.cloned.1.call-done = f32[1024,1024]{1,0:T(8,128)} async-done(((f32[2048,1024]{1,0:T(8,128)}), f32[1024,1024]{1,0:T(8,128)}) %reduce-scatter.26.cloned.1.call-update) | async-done | bytes 4194320 | tf_op jit(solution)/shard_map/reduce_scatter | solution.py:31
  701.4 191.4 %reduce-scatter.22.cloned.1.call-done = f32[1024,2048]{1,0:T(8,128)} async-done(((f32[2048,2048]{1,0:T(8,128)}), f32[1024,2048]{1,0:T(8,128)}) %reduce-scatter.22.cloned.1.call-update) | async-done | bytes 8388624 | tf_op jit(solution)/shard_map/reduce_scatter | solution.py:31
  903.5 103.4 %all-gather.22.cloned.1.call-done = bf16[2048,2048]{1,0:T(8,128)(2,1)} async-done(((bf16[1024,2048]{1,0:T(8,128)(2,1)}), bf16[2048,2048]{1,0:T(8,128)(2,1)}) %all-gather.22.cloned.1.call-update) | async-done | bytes 8388624 | tf_op jit(solution)/shard_map/all_gather | solution.py:27
  1021.6 44.2 %all-gather.18.cloned.1.call-done = bf16[2048,1024]{1,0:T(8,128)(2,1)} async-done(((bf16[1024,1024]{1,0:T(8,128)(2,1)}), bf16[2048,1024]{1,0:T(8,128)(2,1)}) %all-gather.18.cloned.1.call-update) | async-done | bytes 4194320 | tf_op jit(solution)/shard_map/all_gather | solution.py:27
  1074.9 65.3 %reduce-scatter.28.cloned.1.call-done = f32[512,1024]{1,0:T(8,128)} async-done(((f32[2048,1024]{1,0:T(8,128)}), f32[512,1024]{1,0:T(8,128)}) %reduce-scatter.28.cloned.1.call-update) | async-done | bytes 2097168 | tf_op jit(solution)/shard_map/reduce_scatter | solution.py:18
  1148.1 66.3 %reduce-scatter.24.cloned.1.call-done = f32[512,1024]{1,0:T(8,128)} async-done(((f32[2048,1024]{1,0:T(8,128)}), f32[512,1024]{1,0:T(8,128)}) %reduce-scatter.24.cloned.1.call-update) | async-done | bytes 2097168 | tf_op jit(solution)/shard_map/reduce_scatter | solution.py:18
  1219.6 34.6 %all-gather.24.cloned.1.call-done = bf16[2048,1024]{1,0:T(8,128)(2,1)} async-done(((bf16[512,1024]{1,0:T(8,128)(2,1)}), bf16[2048,1024]{1,0:T(8,128)(2,1)}) %all-gather.24.cloned.1.call-update) | async-done | bytes 4194320 | tf_op jit(solution)/shard_map/all_gather | solution.py:14
  1265.4 98.9 %reduce-scatter.30.cloned.1.call-done = f32[2048,512]{1,0:T(8,128)} async-done(((f32[2048,1024]{1,0:T(8,128)}), f32[2048,512]{1,0:T(8,128)}) %reduce-scatter.30.cloned.1.call-update) | async-done | bytes 4194320 | tf_op jit(solution)/shard_map/reduce_scatter | solution.py:225
  1376.5 20.8 while.27
  1408.6 30.5 %all-gather.26.cloned.1.call-done = bf16[2048,512]{1,0:T(8,128)(2,1)} async-done(((bf16[2048,256]{1,0:T(8,128)(2,1)}), bf16[2048,512]{1,0:T(8,128)(2,1)}) %all-gather.26.cloned.1.call-update) | async-done | bytes 2097168 | tf_op jit(solution)/shard_map/all_gather | solution.py:277
  1446.3 51.7 %all-gather.32.cloned.1.call-done = bf16[2048,1024]{1,0:T(8,128)(2,1)} async-done(((bf16[2048,512]{1,0:T(8,128)(2,1)}), bf16[2048,1024]{1,0:T(8,128)(2,1)}) %all-gather.32.cloned.1.call-update) | async-done | bytes 4194320 | tf_op jit(solution)/shard_map/all_gather | solution.py:280
  1507.1 49.7 %all-gather.30.cloned.1.call-done = bf16[2048,1024]{1,0:T(8,128)(2,1)} async-done(((bf16[2048,512]{1,0:T(8,128)(2,1)}), bf16[2048,1024]{1,0:T(8,128)(2,1)}) %all-gather.30.cloned.1.call-update) | async-done | bytes 4194320 | tf_op jit(solution)/shard_map/all_gather | solution.py:279
  1567.7 24.4 all-gather.28.cloned.1.call-done
  1686.1 33.7 %all-reduce = (f32[1024]{0:T(1024)}, f32[1024]{0:T(1024)}) all-reduce(f32[1024]{0:T(1024)S(1)} %get-tuple-element.139, f32[1024]{0:T(1024)S(1)} %copy-done.32), channel_id=1, replica_groups=mesh['dp'=4,'row'=4,'col'=2] {'dp','row'}, use_global_device_ids=true, to_apply=%region_36.37 | all-reduce | flops 2048 | bytes 16384 | tf_op jit(solution)/shard_map/psum | solution.py:296
  1724.1 937.4 %all-reduce.6.cloned.1.call-done = (f32[1024,512]{1,0:T(8,128)}, f32[1024,512]{1,0:T(8,128)}, f32[1024,1024]{1,0:T(8,128)}, f32[1024,1024]{1,0:T(8,128)}, f32[10...) async-done(((f32[1024,512]{1,0:T(8,128)}, f32[1024,512]{1,0:T(8,128)}, f32[1024,1024]{1,0:T(8,128)}, ...) | async-done | bytes 29360144 | tf_op jit(solution)/shard_map/psum | solution.py:307
  (234 shorter events, 408.6 us)
Async XLA Ops:
  7.2 555.9 %copy-start = (bf16[1024,1024]{1,0:T(8,128)(2,1)S(1)}, bf16[1024,1024]{1,0:T(8,128)(2,1)}, u32[]{:S(2)}) copy-start(bf16[1024,1024]{1,0:T(8,128)(2,1)} %param.30) | copy-start | bytes 6291460
  7.2 53.7 %all-gather.12.cloned.1.call-start = ((), (), s32[]{:S(2)}) async-start(), calls=%async_computation.11 | async-start | bytes 5242880 | tf_op jit(solution)/shard_map/all_gather | solution.py:14
  24.5 97.5 %reduce-scatter.16.cloned.1.call-start = ((), (), s32[]{:S(2)}) async-start(), calls=%async_computation.14 | async-start | bytes 6291456 | tf_op jit(solution)/shard_map/reduce_scatter | solution.py:130
  67.5 111.8 %reduce-scatter.14.cloned.1.call-start = ((), (), s32[]{:S(2)}) async-start(), calls=%async_computation.13 | async-start | bytes 6291456 | tf_op jit(solution)/shard_map/reduce_scatter | solution.py:124
  75.3 205.5 %reduce-scatter.18.cloned.1.call-start = ((), (), s32[]{:S(2)}) async-start(), calls=%async_computation.15 | async-start | bytes 12582912 | tf_op jit(solution)/shard_map/reduce_scatter | solution.py:136
  86.0 296.2 %reduce-scatter.12.cloned.1.call-start = ((), (), s32[]{:S(2)}) async-start(), calls=%async_computation.12 | async-start | bytes 12582912 | tf_op jit(solution)/shard_map/reduce_scatter | solution.py:142
  97.1 347.2 %all-gather.14.cloned.1.call-start = ((), (), s32[]{:S(2)}) async-start(), calls=%async_computation.16 | async-start | bytes 6291456 | tf_op jit(solution)/shard_map/all_gather | solution.py:186
  387.5 139.5 %reduce-scatter.20.cloned.1.call-start = ((), (), s32[]{:S(2)}) async-start(), calls=%async_computation.17 | async-start | bytes 10485760 | tf_op jit(solution)/shard_map/reduce_scatter | solution.py:18
  455.1 108.0 %all-gather.20.cloned.1.call-start = ((), (), s32[]{:S(2)}) async-start(), calls=%async_computation.22 | async-start | bytes 5242880 | tf_op jit(solution)/shard_map/all_gather | solution.py:14
  455.8 144.0 %all-gather.16.cloned.1.call-start = ((), (), s32[]{:S(2)}) async-start(), calls=%async_computation.18 | async-start | bytes 5242880 | tf_op jit(solution)/shard_map/all_gather | solution.py:14
  545.1 156.3 %reduce-scatter.26.cloned.1.call-start = ((), (), s32[]{:S(2)}) async-start(), calls=%async_computation.23 | async-start | bytes 12582912 | tf_op jit(solution)/shard_map/reduce_scatter | solution.py:31
  572.1 320.7 %reduce-scatter.22.cloned.1.call-start = ((), (), s32[]{:S(2)}) async-start(), calls=%async_computation.19 | async-start | bytes 25165824 | tf_op jit(solution)/shard_map/reduce_scatter | solution.py:31
  615.0 391.9 %all-gather.22.cloned.1.call-start = ((), (), s32[]{:S(2)}) async-start(), calls=%async_computation.24 | async-start | bytes 12582912 | tf_op jit(solution)/shard_map/all_gather | solution.py:27
  902.7 163.2 %all-gather.18.cloned.1.call-start = ((), (), s32[]{:S(2)}) async-start(), calls=%async_computation.20 | async-start | bytes 6291456 | tf_op jit(solution)/shard_map/all_gather | solution.py:27
  903.4 236.8 %reduce-scatter.28.cloned.1.call-start = ((), (), s32[]{:S(2)}) async-start(), calls=%async_computation.25 | async-start | bytes 10485760 | tf_op jit(solution)/shard_map/reduce_scatter | solution.py:18
  1021.3 193.1 %reduce-scatter.24.cloned.1.call-start = ((), (), s32[]{:S(2)}) async-start(), calls=%async_computation.21 | async-start | bytes 10485760 | tf_op jit(solution)/shard_map/reduce_scatter | solution.py:18
  1074.9 179.3 %all-gather.24.cloned.1.call-start = ((), (), s32[]{:S(2)}) async-start(), calls=%async_computation.26 | async-start | bytes 5242880 | tf_op jit(solution)/shard_map/all_gather | solution.py:14
  1219.6 144.7 %reduce-scatter.30.cloned.1.call-start = ((), (), s32[]{:S(2)}) async-start(), calls=%async_computation.27 | async-start | bytes 12582912 | tf_op jit(solution)/shard_map/reduce_scatter | solution.py:225
  1264.9 174.3 %all-gather.26.cloned.1.call-start = ((), (), s32[]{:S(2)}) async-start(), calls=%async_computation.28 | async-start | bytes 3145728 | tf_op jit(solution)/shard_map/all_gather | solution.py:277
  1405.9 92.2 %all-gather.32.cloned.1.call-start = ((), (), s32[]{:S(2)}) async-start(), calls=%async_computation.31 | async-start | bytes 6291456 | tf_op jit(solution)/shard_map/all_gather | solution.py:280
  1406.7 150.2 %all-gather.30.cloned.1.call-start = ((), (), s32[]{:S(2)}) async-start(), calls=%async_computation.30 | async-start | bytes 6291456 | tf_op jit(solution)/shard_map/all_gather | solution.py:279
  1407.2 184.8 %all-gather.28.cloned.1.call-start = ((), (), s32[]{:S(2)}) async-start(), calls=%async_computation.29 | async-start | bytes 3145728 | tf_op jit(solution)/shard_map/all_gather | solution.py:278
  1408.4 270.2 %reduce-scatter.32.cloned.1.call-start = ((), (), s32[]{:S(2)}) async-start(), calls=%async_computation.32 | async-start | bytes 10485760 | tf_op jit(solution)/shard_map/reduce_scatter | solution.py:18
  1606.8 1054.7 %all-reduce.6.cloned.1.call-start = ((), (), s32[]{:S(2)}) async-start(), calls=%async_computation.33 | async-start | bytes 58720256 | tf_op jit(solution)/shard_map/psum | solution.py:307
  (45 other events, 1183.8 us)
Sparse Core Ops, SparseCore 0:
  24.6 36.2 all-gather.11
  67.6 54.3 reduce-scatter.15
  125.0 54.2 reduce-scatter.13
  181.4 99.2 reduce-scatter.17
  283.0 99.2 reduce-scatter.11
  387.6 56.7 all-gather.13
  455.2 71.7 reduce-scatter.19
  528.6 34.4 all-gather.19
  565.3 34.4 all-gather.15
  602.1 99.2 reduce-scatter.25
  703.7 189.1 reduce-scatter.21
  902.8 104.0 all-gather.21
  1009.0 56.7 all-gather.17
  1068.4 71.7 reduce-scatter.27
  1142.6 71.7 reduce-scatter.23
  1219.7 34.4 all-gather.23
  1265.0 99.2 reduce-scatter.29
  1406.0 33.0 all-gather.25
  1441.3 56.7 all-gather.31
  1500.0 56.7 all-gather.29
  1558.9 33.0 all-gather.27
  1606.9 71.7 reduce-scatter.31
  1683.7 977.7 all-reduce.5
where the time goes:
time: 2700 us; the launch traced here: 2690 us
  waiting for transfers between devices  2250 us (83%)
  matrix products  225 us (8%)
  other arithmetic  84.3 us (3%)
  blocking collectives  76.7 us (3%)
  local copies, waits for them, and re-layouts  39 us (1%)
    psum x1, waiting for transfers between devices, body(): lax.psum((query_grad, key_grad, value_grad, swish_grad, group_gain_part,...  937 us
    reduce_scatter x2, waiting for transfers between devices, share_total(): return lax.psum_scatter(row_block, 'col', scatter_dimension=0, tiled=True)  278 us
    reduce_scatter x4, waiting for transfers between devices, row_total(): lax.psum_scatter(term_fn(jnp.int32(0), row_count * lax.axis_size('row')),...  205 us
    all_gather x2, waiting for transfers between devices, share_gather(): return lax.all_gather(row_block, 'col', axis=0, tiled=True)  148 us
    all_gather x4, waiting for transfers between devices, token_gather(): return lax.all_gather(row_block, 'row', axis=0, tiled=True)  111 us
    reduce_scatter x1, waiting for transfers between devices, body(): lax.psum_scatter(contract_cols(attn_in, output_weight), 'col', scatter_di...  98.9 us
    reduce_scatter x1, waiting for transfers between devices, body(): lax.psum_scatter(jnp.dot(first_full, value_weight, preferred_element_type...  92.8 us
    reduce_scatter x1, waiting for transfers between devices, body(): lax.psum_scatter(jnp.dot(first_full, swish_weight, preferred_element_type...  82.3 us
  transfers between devices with their start and end apart: 23, of which 23 were waited for; matrix products, arithmetic and copies ran while one was open for 8% of the time, Pallas kernels for 0%

commit v1 on v0

v1 whole, which is shorter than its diff:
```python
import jax
import jax.numpy as jnp
from jax import lax
from jax.sharding import PartitionSpec as P

LEN = 1024
EPS = 1e-05
ROTARY_BASE = 10000.0
BF = jnp.bfloat16
F32 = jnp.float32
RC = ("row", "col")


def grid_perm(target):
    pairs = []
    for row in range(4):
        for col in range(2):
            place = target(row // 2, row % 2, col)
            if place is not None:
                pairs.append((row * 2 + col, (place[0] * 2 + place[1]) * 2 + place[2]))
    return pairs


TO_COL = grid_perm(lambda x, k, y: (x, k, 1 - y))
TO_X = grid_perm(lambda x, k, y: (1 - x, k, y))
TO_CORE = grid_perm(lambda x, k, y: (x, 1 - k, y))
SEQ_IN = grid_perm(lambda x, k, y: (1 - x, k, y) if x == y else (x, k, 1 - y))
SEQ_OUT = grid_perm(lambda x, k, y: (x, k, 1 - y) if x == y else (1 - x, k, y))
CROSS = grid_perm(lambda x, k, y: (1 - x, k, 1 - y) if x != y else None)


def move(value, pairs):
    return lax.ppermute(value, RC, pairs)


def dot(left, right):
    return jnp.dot(left, right, preferred_element_type=F32)


def contract_rows(left, right):
    return lax.dot_general(left, right, (((0,), (0,)), ((), ())), preferred_element_type=F32)


def contract_cols(left, right):
    return lax.dot_general(left, right, (((1,), (1,)), ((), ())), preferred_element_type=F32)


def normalize(rows):
    average = jnp.mean(rows, 1, keepdims=True)
    centred = rows - average
    variance = jnp.mean(centred * centred, 1, keepdims=True)
    inverse = lax.rsqrt(variance + EPS)
    return centred * inverse, inverse


def norm_back(grad_rows, normed, inverse, gain):
    scaled = grad_rows * gain
    grad_in = inverse * (
        scaled
        - jnp.mean(scaled, 1, keepdims=True)
        - normed * jnp.mean(scaled * normed, 1, keepdims=True)
    )
    return grad_in, jnp.sum(grad_rows * normed, 0)


def rotate(values, cosine, sine):
    half = values.shape[1] // 2
    front, back = values[:, :half], values[:, half:]
    return jnp.concatenate((front * cosine - back * sine, front * sine + back * cosine), 1)


def rotate_back(values, cosine, sine):
    half = values.shape[1] // 2
    front, back = values[:, :half], values[:, half:]
    return jnp.concatenate((front * cosine + back * sine, back * cosine - front * sine), 1)


def gather_rows(own):
    from_x = move(own, TO_X)
    from_core = move(own, TO_CORE)
    from_both = move(from_x, TO_CORE)
    return jnp.concatenate((own, from_x, from_core, from_both), 0)


def scatter_rows(front, back):
    quarter = front.shape[0] // 2
    half = front + move(back.astype(BF), TO_CORE).astype(F32)
    return half[:quarter] + move(half[quarter:].astype(BF), TO_X).astype(F32)


def partner_block(block, parity):
    half = block.shape[0] // 2
    first = move(lax.dynamic_slice_in_dim(block, parity * half, half, 0), TO_COL)
    count = lax.axis_size("dp")
    second = lax.ppermute(first, "dp", [(i, i ^ 1) for i in range(count)])
    even = parity == 0
    return jnp.concatenate(
        (jnp.where(even, first, second), jnp.where(even, second, first)), 0
    )


def replica_totals(parts):
    count = lax.axis_size("dp")
    if count != 4:
        return [lax.psum(part, "dp").astype(F32) for part in parts]
    place = lax.axis_index("dp")
    outer = (place == 0) | (place == 3)
    n = len(parts)
    totals = [None] * n
    finals = []
    for step in range(n + 2):
        if step < n and step >= 2:
            sent = jnp.where(outer, parts[step], totals[step - 2])
        elif step < n:
            sent = parts[step]
        else:
            sent = totals[step - 2]
        got = lax.ppermute(sent, "dp", [(0, 1), (1, 0), (2, 3), (3, 2)])
        if step >= 2:
            finals.append(jnp.where(outer, got, totals[step - 2]).astype(F32))
        if step < n:
            local = lax.optimization_barrier(
                (parts[step].astype(F32) + got.astype(F32)).astype(BF)
            )
            other = lax.ppermute(local, "dp", [(1, 2), (2, 1)])
            totals[step] = lax.optimization_barrier(
                (local.astype(F32) + other.astype(F32)).astype(BF)
            )
    return finals


def body(
    tokens,
    grad_out,
    first_gain,
    query_weight,
    key_weight,
    value_weight,
    swish_weight,
    group_gain,
    output_weight,
    second_gain,
    gate_weight,
    up_weight,
    down_weight,
    decay_rate,
):
    row = lax.axis_index("row")
    y = lax.axis_index("col")
    place = lax.axis_index("dp")
    x, k = row // 2, row % 2
    parity = place % 2
    same = x == y
    rows_dev, width = tokens.shape
    quarter = rows_dev // 2

    def sequence_rows(block):
        got = move(block, SEQ_IN)
        cross = move(block, CROSS)
        mine = jnp.where(same, block, got)
        other = jnp.where(same, got, cross)
        both = jnp.concatenate((mine, other), 1)
        return jnp.concatenate(
            (
                lax.dynamic_slice_in_dim(both, x * quarter, quarter, 0),
                lax.dynamic_slice_in_dim(both, (1 - x) * quarter, quarter, 0),
            ),
            0,
        )

    def home(rows):
        mine, other = rows[:, :width], rows[:, width:]
        got = move(jnp.where(same, other, mine).astype(BF), SEQ_OUT)
        cross = move(other.astype(BF), CROSS)
        here = jnp.where(same, mine, got.astype(rows.dtype))
        there = jnp.where(same, got, cross).astype(rows.dtype)
        return jnp.where(
            x == 0, jnp.concatenate((here, there), 0), jnp.concatenate((there, here), 0)
        )

    head_values = group_gain.shape[0]
    small = jnp.concatenate((first_gain, second_gain, group_gain, decay_rate))
    small_other = move(small, TO_COL)
    first_gain_full = jnp.concatenate((first_gain, small_other[:width]))
    second_gain_full = jnp.concatenate((second_gain, small_other[width : 2 * width]))
    own_group = (group_gain, small_other[2 * width : 2 * width + head_values])
    own_rate = (decay_rate[0], small_other[2 * width + head_values])
    group_gains = tuple(jnp.where(y == 0, own_group[i], own_group[1 - i]) for i in range(2))
    rates = tuple(jnp.where(y == 0, own_rate[i], own_rate[1 - i]) for i in range(2))

    input_half = sequence_rows(tokens)
    weights = {}
    query_other = partner_block(query_weight, parity)
    key_other = partner_block(key_weight, parity)
    value_other = partner_block(value_weight, parity)
    swish_other = partner_block(swish_weight, parity)
    output_other = partner_block(output_weight, parity)
    gate_other = partner_block(gate_weight, parity)
    up_other = partner_block(up_weight, parity)
    down_other = partner_block(down_weight, parity)

    input_rows = input_half.astype(F32)
    half_normed, half_inv = normalize(input_rows)
    first_half = (half_normed * first_gain_full).astype(BF)
    first_in = jnp.concatenate((first_half, move(first_half, TO_CORE)), 0)
    own_input = input_rows[:quarter]
    first_normed, first_inv = half_normed[:quarter], half_inv[:quarter]
    grad_half = sequence_rows(grad_out)
    grad_rows = jnp.concatenate((grad_half, move(grad_half, TO_CORE)), 0)
    own_grad = grad_half[:quarter].astype(F32)

    def project(rows, mine, other):
        return dot(rows[:, :width], mine) + dot(rows[:, width:], other)

    queries = project(first_in, query_weight, query_other)
    keys_pre = project(first_in, key_weight, key_other)
    valued = project(first_in, value_weight, value_other).astype(BF)
    swish_in = project(first_in, swish_weight, swish_other)

    base = 2 * k + x
    block_ids = jnp.bitwise_xor(base, jnp.arange(4, dtype=jnp.int32))
    positions = (
        block_ids[:, None] * quarter + jnp.arange(quarter, dtype=jnp.int32)[None, :]
    ).reshape(-1)
    key_size = queries.shape[1] // 2
    value_size = valued.shape[1] // 2
    half_key = key_size // 2
    frequency = ROTARY_BASE ** (-jnp.arange(half_key, dtype=F32) / half_key)
    rotation = positions.astype(F32)[:, None] * frequency[None, :]
    cosine, sine = jnp.cos(rotation), jnp.sin(rotation)
    distance = positions[:, None] - positions[None, :]
    lag = jnp.maximum(distance, 0).astype(F32)

    saved = []
    gated_heads = []
    for head in range(2):
        mask = jnp.where(distance >= 0, jnp.exp(-rates[head] * lag), 0.0)
        keys = slice(head * key_size, (head + 1) * key_size)
        values = slice(head * value_size, (head + 1) * value_size)
        query_rot = rotate(queries[:, keys], cosine, sine).astype(BF)
        key_rot = rotate(keys_pre[:, keys], cosine, sine).astype(BF)
        value_low = valued[:, values]
        scores = (contract_cols(query_rot, key_rot) * mask).astype(BF)
        retained = dot(scores, value_low)
        average = jnp.mean(retained, 1, keepdims=True)
        centred = retained - average
        variance = jnp.mean(centred * centred, 1, keepdims=True)
        floor_open = (variance > 1.0).astype(F32)
        group_inv = lax.rsqrt(jnp.maximum(variance, 1.0))
        normed_o = centred * group_inv
        swish_out, swish_pull = jax.vjp(jax.nn.silu, swish_in[:, values])
        gated_heads.append((swish_out * normed_o * group_gains[head]).astype(BF))
        saved.append(
            (mask, query_rot, key_rot, value_low, scores, floor_open, group_inv, normed_o, swish_out, swish_pull)
        )
    gated = jnp.concatenate(gated_heads, 1)

    half_rows = 2 * quarter

    def project_scatter(rows, mine, other):
        back, front = rows[half_rows:], rows[:half_rows]
        back = jnp.concatenate((dot(back, mine), dot(back, other)), 1)
        front = jnp.concatenate((dot(front, mine), dot(front, other)), 1)
        return scatter_rows(front, back)

    x_mid = own_input + project_scatter(gated, output_weight, output_other)
    second_normed, second_inv = normalize(x_mid)
    second_in = gather_rows((second_normed * second_gain_full).astype(BF))
    gate_pre = project(second_in, gate_weight, gate_other)
    up_pre = project(second_in, up_weight, up_other)
    gelu_val, gelu_pull = jax.vjp(jax.nn.gelu, gate_pre)
    hidden = (gelu_val * up_pre).astype(BF)

    def split_grad(left, right):
        return contract_rows(left[:, :width], right), contract_rows(left[:, width:], right)

    def col_total(mine, other):
        return (mine + move(other.astype(BF), TO_COL).astype(F32)).astype(BF)

    def width_grad_in(left, right):
        other = contract_rows(left[:, width:], right)
        return col_total(contract_rows(left[:, :width], right), other)

    def width_grad_out(left, right):
        other = contract_rows(left, right[:, width:])
        return col_total(contract_rows(left, right[:, :width]), other)

    down_part = width_grad_out(hidden, grad_rows)
    grad_hidden = contract_cols(grad_rows[:, :width], down_weight) + contract_cols(
        grad_rows[:, width:], down_other
    )
    grad_gate = gelu_pull(grad_hidden * up_pre)[0].astype(BF)
    grad_up = (grad_hidden * gelu_val).astype(BF)

    def back_scatter(terms):
        def total(rows):
            out = []
            for side in (1, 2):
                part = None
                for term in terms:
                    value = contract_cols(term[0][rows], term[side])
                    part = value if part is None else part + value
                out.append(part)
            return jnp.concatenate(out, 1)

        return scatter_rows(total(slice(0, half_rows)), total(slice(half_rows, None)))

    grad_second = back_scatter(
        ((grad_gate, gate_weight, gate_other), (grad_up, up_weight, up_other))
    )
    gate_part = width_grad_in(second_in, grad_gate)
    up_part = width_grad_in(second_in, grad_up)
    grad_norm_mid, second_gain_part = norm_back(
        grad_second, second_normed, second_inv, second_gain_full
    )
    grad_mid = own_grad + grad_norm_mid
    block_out = home((x_mid + project_scatter(hidden, down_weight, down_other)).astype(BF))

    attn_in = gather_rows(grad_mid.astype(BF))
    grad_gated = contract_cols(attn_in[:, :width], output_weight) + contract_cols(
        attn_in[:, width:], output_other
    )
    output_part = width_grad_out(gated, attn_in)

    grad_queries, grad_keys, grad_values, grad_swishes, group_gain_parts = [], [], [], [], []
    for head in range(2):
        (mask, query_rot, key_rot, value_low, scores, floor_open, group_inv, normed_o, swish_out, swish_pull) = saved[head]
        values = slice(head * value_size, (head + 1) * value_size)
        grad_head = grad_gated[:, values]
        group_gain_parts.append(jnp.sum(grad_head * swish_out * normed_o, 0))
        product = grad_head * group_gains[head]
        grad_normed = product * swish_out
        grad_swishes.append(swish_pull(product * normed_o)[0].astype(BF))
        grad_retained = (
            group_inv
            * (
                grad_normed
                - jnp.mean(grad_normed, 1, keepdims=True)
                - floor_open * normed_o * jnp.mean(grad_normed * normed_o, 1, keepdims=True)
            )
        ).astype(BF)
        grad_values.append(contract_rows(scores, grad_retained).astype(BF))
        grad_scores = (contract_cols(grad_retained, value_low) * mask).astype(BF)
        grad_queries.append(rotate_back(dot(grad_scores, key_rot), cosine, sine).astype(BF))
        grad_keys.append(
            rotate_back(contract_rows(grad_scores, query_rot), cosine, sine).astype(BF)
        )
    grad_query = jnp.concatenate(grad_queries, 1)
    grad_key = jnp.concatenate(grad_keys, 1)
    grad_value = jnp.concatenate(grad_values, 1)
    grad_swish = jnp.concatenate(grad_swishes, 1)

    swish_part = width_grad_in(first_in, grad_swish)
    value_part = width_grad_in(first_in, grad_value)
    query_key_part = width_grad_in(first_in, jnp.concatenate((grad_query, grad_key), 1))

    down_grad, gate_grad, up_grad, output_grad, swish_grad, value_grad, query_key_grad = (
        replica_totals(
            [down_part, gate_part, up_part, output_part, swish_part, value_part, query_key_part]
        )
    )
    head_cols = query_weight.shape[1]
    query_grad, key_grad = query_key_grad[:, :head_cols], query_key_grad[:, head_cols:]

    grad_first = back_scatter(
        (
            (grad_query, query_weight, query_other),
            (grad_key, key_weight, key_other),
            (grad_value, value_weight, value_other),
            (grad_swish, swish_weight, swish_other),
        )
    )
    grad_norm_in, first_gain_part = norm_back(
        grad_first, first_normed, first_inv, first_gain_full
    )
    input_grad = home(grad_mid + grad_norm_in)

    group_pair = jnp.where(
        y == 0,
        jnp.stack(group_gain_parts),
        jnp.stack(group_gain_parts[::-1]),
    )
    outgoing = jnp.concatenate((first_gain_part[width:], second_gain_part[width:], group_pair[1]))
    incoming = move(outgoing, TO_COL)
    gains = jnp.concatenate((first_gain_part[:width], second_gain_part[:width])) + incoming[: 2 * width]
    group_own = group_pair[0] + incoming[2 * width :]
    rows = lax.axis_size("row")
    placed = jnp.where(jnp.arange(rows)[:, None] == row, group_own[None, :], 0.0).reshape(-1)
    gains = lax.psum(jnp.concatenate((gains, placed)), ("dp", "row"))
    group_gain_grad = lax.dynamic_slice_in_dim(gains[2 * width :], row * head_values, head_values)
    return (
        block_out,
        input_grad,
        gains[:width],
        query_grad,
        key_grad,
        value_grad,
        swish_grad,
        group_gain_grad,
        output_grad,
        gains[width : 2 * width],
        gate_grad,
        up_grad,
        down_grad,
    )


def solution(mesh):
    placed = (
        P(("dp", "row"), "col"),
        P(("dp", "row"), "col"),
        P("col"),
        P("col", "row"),
        P("col", "row"),
        P("col", "row"),
        P("col", "row"),
        P(("row", "col")),
        P("row", "col"),
        P("col"),
        P("col", "row"),
        P("col", "row"),
        P("row", "col"),
        P(("row", "col")),
    )
    return jax.shard_map(
        body,
        mesh=mesh,
        in_specs=placed,
        out_specs=(
            P(("dp", "row"), "col"),
            P(("dp", "row"), "col"),
            P("col"),
            P("col", "row"),
            P("col", "row"),
            P("col", "row"),
            P("col", "row"),
            P(("row", "col")),
            P("row", "col"),
            P("col"),
            P("col", "row"),
            P("col", "row"),
            P("row", "col"),
        ),
        check_vma=False,
    )
```

time: 2700 us -> 1070 us (0.40)
  waiting for transfers between devices: 2250 us -> 470 us
  starting transfers between devices: 2.73 us -> 148 us
  other arithmetic: 84.3 us -> 120 us
  matrix products: 225 us -> 192 us
    psum x1 -> x0, waiting for transfers between devices: 937 us -> none  [body(): lax.psum((query_grad, key_grad, value_grad, swish_grad, group_gain_part,...]
    reduce_scatter x11 -> x0, waiting for transfers between devices: 838 us -> none  [the longest x2 278 us: share_total(): return lax.psum_scatter(row_block, 'col', scatter_dimension=0, tiled=True)]
    all_gather x11 -> x0, waiting for transfers between devices: 472 us -> none  [the longest x2 148 us: share_gather(): return lax.all_gather(row_block, 'col', axis=0, tiled=True)]
    ppermute x0 -> x65, waiting for transfers between devices: none -> 470 us  [the longest x41 244 us: move(): return lax.ppermute(value, RC, pairs)]
    ppermute x0 -> x65, starting transfers between devices: none -> 148 us  [the longest x9 80.6 us: replica_totals(): got = lax.ppermute(sent, 'dp', [(0, 1), (1, 0), (2, 3), (3, 2)])]
    dot_general x17 -> x24, matrix products: 99.5 us -> 57.6 us  [dot(): return jnp.dot(left, right, preferred_element_type=F32)]
    dot_general x7 -> x18, matrix products: 49.3 us -> 71.1 us  [contract_rows(): lax.dot_general(left, right, (((0,), (0,)), ((), ())), preferred_element_...]
    dot_general x7 -> x32, matrix products: 75.9 us -> 63 us  [contract_cols(): lax.dot_general(left, right, (((1,), (1,)), ((), ())), preferred_element_...]
  transfers between devices with their start and end apart: 23 -> 65, of which waited for: 23 -> 24; matrix products, arithmetic and copies ran while one was open for 8% -> 24% of each run, Pallas kernels for 0% -> 0%
where the time goes in v1:
time: 1070 us; the launch traced here: 1060 us
  waiting for transfers between devices  470 us (44%)
  matrix products  192 us (18%)
  starting transfers between devices  148 us (14%)
  other arithmetic  120 us (11%)
  blocking collectives  86.9 us (8%)
  local copies, waits for them, and re-layouts  38.1 us (4%)
    ppermute x41, waiting for transfers between devices, move(): return lax.ppermute(value, RC, pairs)  244 us
    ppermute x9, waiting for transfers between devices, replica_totals(): got = lax.ppermute(sent, 'dp', [(0, 1), (1, 0), (2, 3), (3, 2)])  189 us
    psum x1, blocking collectives, body(): gains = lax.psum(jnp.concatenate((gains, placed)), ('dp', 'row'))  86.9 us
    ppermute x9, starting transfers between devices, replica_totals(): got = lax.ppermute(sent, 'dp', [(0, 1), (1, 0), (2, 3), (3, 2)])  80.6 us
    dot_general x18, matrix products, contract_rows(): lax.dot_general(left, right, (((0,), (0,)), ((), ())), preferred_element_...  71.1 us
    dot_general x32, matrix products, contract_cols(): lax.dot_general(left, right, (((1,), (1,)), ((), ())), preferred_element_...  63 us
    dot_general x24, matrix products, dot(): return jnp.dot(left, right, preferred_element_type=F32)  57.6 us
    ppermute x41, starting transfers between devices, move(): return lax.ppermute(value, RC, pairs)  44.8 us
  transfers between devices with their start and end apart: 65, of which 24 were waited for; matrix products, arithmetic and copies ran while one was open for 24% of the time, Pallas kernels for 0%

profile of v1, /device:TPU:0, one launch (start us, length us, event | category | flops | bytes accessed | tf_op | source)
XLA Modules:
  0.0 1060.5 jit_solution(10906418812323513875)
XLA Ops:
  18.5 31.3 %collective-permute-done.2 = f32[2561]{0:T(1024)S(1)} collective-permute-done((f32[2561]{0:T(1024)S(1)}, f32[2561]{0:T(1024)S(1)}, u32[]{:S(2)}, u32[]{:S(2)}) %collective-permute-start.2) | collective-permute-done | bytes 10276 | tf_op jit(solution)/shard_map/ppermute | solution.py:33
  56.9 10.0 collective-permute-done.8
  81.9 22.5 %collective-permute-done.10 = bf16[512,1024]{1,0:T(8,128)(2,1)} collective-permute-done((bf16[512,1024]{1,0:T(8,128)(2,1)}, bf16[512,1024]{1,0:T(8,128)(2,1)}, u32[]{:S(2)}, u32[]{:S(2)}) %collective-permute-start.10) | collective-permute-done | bytes 1048608 | tf_op jit(solution)/shard_map/ppermute | solution.py:33
  108.3 18.5 %collective-permute-done.4 = bf16[512,1024]{1,0:T(8,128)(2,1)} collective-permute-done((bf16[512,1024]{1,0:T(8,128)(2,1)}, bf16[512,1024]{1,0:T(8,128)(2,1)}, u32[]{:S(2)}, u32[]{:S(2)}) %collective-permute-start.4) | collective-permute-done | bytes 1048608 | tf_op jit(solution)/shard_map/ppermute | solution.py:33
  128.6 19.1 %collective-permute-done.12 = bf16[512,1024]{1,0:T(8,128)(2,1)} collective-permute-done((bf16[512,1024]{1,0:T(8,128)(2,1)}, bf16[512,1024]{1,0:T(8,128)(2,1)}, u32[]{:S(2)}, u32[]{:S(2)}) %collective-permute-start.12) | collective-permute-done | bytes 1048608 | tf_op jit(solution)/shard_map/ppermute | solution.py:33
  154.6 9.8 collective-permute-done.5
  165.7 17.1 %collective-permute-done.13 = bf16[512,1024]{1,0:T(8,128)(2,1)S(1)} collective-permute-done((bf16[512,1024]{1,0:T(8,128)(2,1)}, bf16[512,1024]{1,0:T(8,128)(2,1)S(1)}, u32[]{:S(2)}, u32[]{:S(2)}) %collective-permute-start.13) | collective-permute-done | bytes 1048608 | tf_op jit(solution)/shard_map/ppermute | solution.py:95
  227.0 20.6 %collective-permute-done.19 = bf16[512,1024]{1,0:T(8,128)(2,1)} collective-permute-done((bf16[512,1024]{1,0:T(8,128)(2,1)}, bf16[512,1024]{1,0:T(8,128)(2,1)}, u32[]{:S(2)}, u32[]{:S(2)}) %collective-permute-start.19) | collective-permute-done | bytes 1048608 | tf_op jit(solution)/shard_map/ppermute | solution.py:33
  249.3 20.7 %collective-permute-done.21 = bf16[512,1024]{1,0:T(8,128)(2,1)} collective-permute-done((bf16[512,1024]{1,0:T(8,128)(2,1)}, bf16[512,1024]{1,0:T(8,128)(2,1)}, u32[]{:S(2)}, u32[]{:S(2)}) %collective-permute-start.21) | collective-permute-done | bytes 1048608 | tf_op jit(solution)/shard_map/ppermute | solution.py:33
  282.2 9.9 collective-permute-done.23
  307.4 9.7 collective-permute-done.24
  345.2 10.4 fusion.21
  402.4 14.9 %collective-permute-done.45 = bf16[1024,1024]{1,0:T(8,128)(2,1)S(1)} collective-permute-done((bf16[1024,1024]{1,0:T(8,128)(2,1)S(1)}, bf16[1024,1024]{1,0:T(8,128)(2,1)S(1)}, u32[]{:S(2)}, u32[]{:S(2)}) %collective-permute-start.45) | collective-permute-done | bytes 2097184 | tf_op jit(solution)/shard_map/ppermute | solution.py:33
  426.5 35.4 %collective-permute-done.57 = bf16[1024,1024]{1,0:T(8,128)(2,1)} collective-permute-done((bf16[1024,1024]{1,0:T(8,128)(2,1)}, bf16[1024,1024]{1,0:T(8,128)(2,1)}, u32[]{:S(2)}, u32[]{:S(2)}) %collective-permute-start.57) | collective-permute-done | bytes 2097184 | tf_op jit(solution)/shard_map/ppermute | solution.py:33
  480.6 26.8 %collective-permute-done.27 = bf16[256,1024]{1,0:T(8,128)(2,1)S(1)} collective-permute-done((bf16[256,1024]{1,0:T(8,128)(2,1)S(1)}, bf16[256,1024]{1,0:T(8,128)(2,1)S(1)}, u32[]{:S(2)}, u32[]{:S(2)}) %collective-permute-start.27) | collective-permute-done | bytes 524320 | tf_op jit(solution)/shard_map/ppermute | solution.py:33
  618.9 36.4 %collective-permute-done.48 = bf16[1024,1024]{1,0:T(8,128)(2,1)S(1)} collective-permute-done((bf16[1024,1024]{1,0:T(8,128)(2,1)}, bf16[1024,1024]{1,0:T(8,128)(2,1)S(1)}, u32[]{:S(2)}, u32[]{:S(2)}) %collective-permute-start.48) | collective-permute-done | bytes 2097184 | tf_op jit(solution)/shard_map/ppermute | solution.py:118
  676.0 6.9 broadcast_select_fusion.3
  682.9 30.3 %collective-permute-start.50 = (bf16[1024,1024]{1,0:T(8,128)(2,1)}, bf16[1024,1024]{1,0:T(8,128)(2,1)S(1)}, u32[]{:S(2)}, u32[]{:S(2)}) collective-permute-start(bf16[1024,1024]{1,0:T(8,128)(2,1)} %get-tuple-element.119), channel_id=1, source_target_pairs={{0,8},{8,0},{16,24},{24,16},{1,9},{9,1},{17,25},{25,17},{2,10},{10... | collective-permute-start | bytes 6291464 | tf_op jit(solution)/shard_map/ppermute | solution.py:118
  727.7 35.4 %collective-permute-done.50 = bf16[1024,1024]{1,0:T(8,128)(2,1)S(1)} collective-permute-done((bf16[1024,1024]{1,0:T(8,128)(2,1)}, bf16[1024,1024]{1,0:T(8,128)(2,1)S(1)}, u32[]{:S(2)}, u32[]{:S(2)}) %collective-permute-start.50) | collective-permute-done | bytes 2097184 | tf_op jit(solution)/shard_map/ppermute | solution.py:118
  786.2 36.9 %collective-permute-start.52 = (bf16[1024,1024]{1,0:T(8,128)(2,1)}, bf16[1024,1024]{1,0:T(8,128)(2,1)S(1)}, u32[]{:S(2)}, u32[]{:S(2)}) collective-permute-start(bf16[1024,1024]{1,0:T(8,128)(2,1)} %get-tuple-element.121), channel_id=1, source_target_pairs={{0,8},{8,0},{16,24},{24,16},{1,9},{9,1},{17,25},{25,17},{2,10},{10... | collective-permute-start | bytes 6291464 | tf_op jit(solution)/shard_map/ppermute | solution.py:118
  832.5 36.7 %collective-permute-done.52 = bf16[1024,1024]{1,0:T(8,128)(2,1)S(1)} collective-permute-done((bf16[1024,1024]{1,0:T(8,128)(2,1)}, bf16[1024,1024]{1,0:T(8,128)(2,1)S(1)}, u32[]{:S(2)}, u32[]{:S(2)}) %collective-permute-start.52) | collective-permute-done | bytes 2097184 | tf_op jit(solution)/shard_map/ppermute | solution.py:118
  873.6 86.9 %psum.7 = f32[4096]{0:T(1024)S(1)} all-reduce(f32[4096]{0:T(1024)S(1)} %pad_maximum_fusion.69), channel_id=1, replica_groups=mesh['dp'=4,'row'=4,'col'=2] {'dp','row'}, use_global_device_ids=true, to_apply=%region_20.21 | all-reduce | flops 4096 | bytes 32768 | tf_op jit(solution)/shard_map/psum | solution.py:389
  983.8 31.2 %collective-permute-done.64 = bf16[1024,1024]{1,0:T(8,128)(2,1)S(1)} collective-permute-done((bf16[1024,1024]{1,0:T(8,128)(2,1)S(1)}, bf16[1024,1024]{1,0:T(8,128)(2,1)S(1)}, u32[]{:S(2)}, u32[]{:S(2)}) %collective-permute-start.64) | collective-permute-done | bytes 2097184 | tf_op jit(solution)/shard_map/ppermute | solution.py:118
  1017.3 40.2 %collective-permute-done.54 = bf16[1024,1024]{1,0:T(8,128)(2,1)S(1)} collective-permute-done((bf16[1024,1024]{1,0:T(8,128)(2,1)S(1)}, bf16[1024,1024]{1,0:T(8,128)(2,1)S(1)}, u32[]{:S(2)}, u32[]{:S(2)}) %collective-permute-start.54) | collective-permute-done | bytes 2097184 | tf_op jit(solution)/shard_map/ppermute | solution.py:118
  (618 shorter events, 437.6 us)
Async XLA Ops:
  0.7 68.0 %collective-permute-start = (bf16[512,1024]{1,0:T(8,128)(2,1)}, bf16[512,1024]{1,0:T(8,128)(2,1)}, u32[]{:S(2)}, u32[]{:S(2)}) collective-permute-start(bf16[512,1024]{1,0:T(8,128)(2,1)} %param.14), channel_id=1, source_target_pairs={{0,4},{1,0},{2,6},{3,2},{4,5},{5,1},{6,7},{7,3},{8,12},{9,8},{10,1... | collective-permute-start | bytes 3145736 | tf_op jit(solution)/shard_map/ppermute | solution.py:33
  3.7 65.3 %collective-permute-start.1 = (bf16[512,1024]{1,0:T(8,128)(2,1)}, bf16[512,1024]{1,0:T(8,128)(2,1)}, u32[]{:S(2)}, u32[]{:S(2)}) collective-permute-start(bf16[512,1024]{1,0:T(8,128)(2,1)} %param.14), channel_id=1, source_target_pairs={{1,4},{3,6},{4,1},{6,3},{9,12},{11,14},{12,9},{14,11},{17,20},{19,... | collective-permute-start | bytes 3145736 | tf_op jit(solution)/shard_map/ppermute | solution.py:33
  5.3 65.4 %collective-permute-start.29 = (bf16[512,1024]{1,0:T(8,128)(2,1)}, bf16[512,1024]{1,0:T(8,128)(2,1)}, u32[]{:S(2)}, u32[]{:S(2)}) collective-permute-start(bf16[512,1024]{1,0:T(8,128)(2,1)} %param.15), channel_id=1, source_target_pairs={{0,4},{1,0},{2,6},{3,2},{4,5},{5,1},{6,7},{7,3},{8,12},{9,8},{10,1... | collective-permute-start | bytes 3145736 | tf_op jit(solution)/shard_map/ppermute | solution.py:33
  7.3 63.7 %collective-permute-start.30 = (bf16[512,1024]{1,0:T(8,128)(2,1)}, bf16[512,1024]{1,0:T(8,128)(2,1)}, u32[]{:S(2)}, u32[]{:S(2)}) collective-permute-start(bf16[512,1024]{1,0:T(8,128)(2,1)} %param.15), channel_id=1, source_target_pairs={{1,4},{3,6},{4,1},{6,3},{9,12},{11,14},{12,9},{14,11},{17,20},{19,... | collective-permute-start | bytes 3145736 | tf_op jit(solution)/shard_map/ppermute | solution.py:33
  70.7 77.0 %collective-permute-start.12 = (bf16[512,1024]{1,0:T(8,128)(2,1)}, bf16[512,1024]{1,0:T(8,128)(2,1)}, u32[]{:S(2)}, u32[]{:S(2)}) collective-permute-start(bf16[512,1024]{1,0:T(8,128)(2,1)} %constant_dynamic-slice_fusion.3), channel_id=1, source_target_pairs={{0,1},{1,0},{2,3},{3,2},{4,5},{5,4},{6,7},{7,6},{8,9},{9,8},{10,11... | collective-permute-start | bytes 3145736 | tf_op jit(solution)/shard_map/ppermute | solution.py:33
  81.9 102.5 %collective-permute-start.3 = (bf16[512,2048]{1,0:T(8,128)(2,1)}, bf16[512,2048]{1,0:T(8,128)(2,1)}, u32[]{:S(2)}, u32[]{:S(2)}) collective-permute-start(bf16[512,2048]{1,0:T(8,128)(2,1)} %get-tuple-element.67), channel_id=1, source_target_pairs={{0,2},{1,3},{2,0},{3,1},{4,6},{5,7},{6,4},{7,5},{8,10},{9,11},{10,... | collective-permute-start | bytes 6291464 | tf_op jit(solution)/shard_map/ppermute | solution.py:33
  225.4 66.7 %collective-permute-start.23 = (bf16[512,1024]{1,0:T(8,128)(2,1)}, bf16[512,1024]{1,0:T(8,128)(2,1)}, u32[]{:S(2)}, u32[]{:S(2)}) collective-permute-start(bf16[512,1024]{1,0:T(8,128)(2,1)} %constant_dynamic-slice_fusion), channel_id=1, source_target_pairs={{0,1},{1,0},{2,3},{3,2},{4,5},{5,4},{6,7},{7,6},{8,9},{9,8},{10,11... | collective-permute-start | bytes 3145736 | tf_op jit(solution)/shard_map/ppermute | solution.py:33
  395.8 66.2 %collective-permute-start.57 = (bf16[1024,1024]{1,0:T(8,128)(2,1)}, bf16[1024,1024]{1,0:T(8,128)(2,1)}, u32[]{:S(2)}, u32[]{:S(2)}) collective-permute-start(bf16[1024,1024]{1,0:T(8,128)(2,1)} %convolution_convert_fusion), channel_id=1, source_target_pairs={{0,1},{1,0},{2,3},{3,2},{4,5},{5,4},{6,7},{7,6},{8,9},{9,8},{10,11... | collective-permute-start | bytes 6291464 | tf_op jit(solution)/shard_map/ppermute | solution.py:33
  419.8 88.4 %collective-permute-start.46 = (bf16[1024,1024]{1,0:T(8,128)(2,1)S(1)}, bf16[1024,1024]{1,0:T(8,128)(2,1)S(1)}, u32[]{:S(2)}, u32[]{:S(2)}) collective-permute-start(bf16[1024,1024]{1,0:T(8,128)(2,1)S(1)} %add_convert_fusion.17), channel_id=1, source_target_pairs={{0,8},{8,0},{16,24},{24,16},{1,9},{9,1},{17,25},{25,17},{2,10},{10... | collective-permute-start | bytes 6291464 | tf_op jit(solution)/shard_map/ppermute | solution.py:118
  479.5 122.5 %collective-permute-start.44 = (bf16[1024,1024]{1,0:T(8,128)(2,1)}, bf16[1024,1024]{1,0:T(8,128)(2,1)}, u32[]{:S(2)}, u32[]{:S(2)}) collective-permute-start(bf16[1024,1024]{1,0:T(8,128)(2,1)} %convolution_convert_fusion.4), channel_id=1, source_target_pairs={{0,1},{1,0},{2,3},{3,2},{4,5},{5,4},{6,7},{7,6},{8,9},{9,8},{10,11... | collective-permute-start | bytes 6291464 | tf_op jit(solution)/shard_map/ppermute | solution.py:33
  514.9 82.5 %collective-permute-start.47 = (bf16[1024,1024]{1,0:T(8,128)(2,1)S(1)}, bf16[1024,1024]{1,0:T(8,128)(2,1)}, u32[]{:S(2)}, u32[]{:S(2)}) collective-permute-start(bf16[1024,1024]{1,0:T(8,128)(2,1)S(1)} %add_convert_fusion.16), channel_id=1, source_target_pairs={{8,16},{16,8},{9,17},{17,9},{10,18},{18,10},{11,19},{19,11},{12,20... | collective-permute-start | bytes 6291464 | tf_op jit(solution)/shard_map/ppermute | solution.py:125
  520.1 139.3 %collective-permute-start.59 = (bf16[1024,1024]{1,0:T(8,128)(2,1)S(1)}, bf16[1024,1024]{1,0:T(8,128)(2,1)}, u32[]{:S(2)}, u32[]{:S(2)}) collective-permute-start(bf16[1024,1024]{1,0:T(8,128)(2,1)S(1)} %add_convert_fusion.5), channel_id=1, source_target_pairs={{8,16},{16,8},{9,17},{17,9},{10,18},{18,10},{11,19},{19,11},{12,20... | collective-permute-start | bytes 6291464 | tf_op jit(solution)/shard_map/ppermute | solution.py:125
  563.3 112.6 %collective-permute-start.43 = (bf16[1024,1024]{1,0:T(8,128)(2,1)}, bf16[1024,1024]{1,0:T(8,128)(2,1)}, u32[]{:S(2)}, u32[]{:S(2)}) collective-permute-start(bf16[1024,1024]{1,0:T(8,128)(2,1)} %convolution_convert_fusion.5), channel_id=1, source_target_pairs={{0,1},{1,0},{2,3},{3,2},{4,5},{5,4},{6,7},{7,6},{8,9},{9,8},{10,11... | collective-permute-start | bytes 6291464 | tf_op jit(solution)/shard_map/ppermute | solution.py:33
  567.9 94.1 %collective-permute-start.56 = (bf16[1024,1024]{1,0:T(8,128)(2,1)}, bf16[1024,1024]{1,0:T(8,128)(2,1)}, u32[]{:S(2)}, u32[]{:S(2)}) collective-permute-start(bf16[1024,1024]{1,0:T(8,128)(2,1)} %convolution_convert_fusion.1), channel_id=1, source_target_pairs={{0,1},{1,0},{2,3},{3,2},{4,5},{5,4},{6,7},{7,6},{8,9},{9,8},{10,11... | collective-permute-start | bytes 6291464 | tf_op jit(solution)/shard_map/ppermute | solution.py:33
  597.5 171.0 %collective-permute-start.55 = (bf16[1024,1024]{1,0:T(8,128)(2,1)}, bf16[1024,1024]{1,0:T(8,128)(2,1)}, u32[]{:S(2)}, u32[]{:S(2)}) collective-permute-start(bf16[1024,1024]{1,0:T(8,128)(2,1)} %convolution_convert_fusion.2), channel_id=1, source_target_pairs={{0,1},{1,0},{2,3},{3,2},{4,5},{5,4},{6,7},{7,6},{8,9},{9,8},{10,11... | collective-permute-start | bytes 6291464 | tf_op jit(solution)/shard_map/ppermute | solution.py:33
  659.4 61.4 %collective-permute-start.37 = (bf16[512,2048]{1,0:T(8,128)(2,1)}, bf16[512,2048]{1,0:T(8,128)(2,1)S(1)}, u32[]{:S(2)}, u32[]{:S(2)}) collective-permute-start(bf16[512,2048]{1,0:T(8,128)(2,1)} %pad_maximum_fusion.18), channel_id=1, source_target_pairs={{0,2},{1,3},{2,0},{3,1},{4,6},{5,7},{6,4},{7,5},{8,10},{9,11},{10,... | collective-permute-start | bytes 6291464 | tf_op jit(solution)/shard_map/ppermute | solution.py:33
  682.9 80.2 %collective-permute-start.50 = (bf16[1024,1024]{1,0:T(8,128)(2,1)}, bf16[1024,1024]{1,0:T(8,128)(2,1)S(1)}, u32[]{:S(2)}, u32[]{:S(2)}) collective-permute-start(bf16[1024,1024]{1,0:T(8,128)(2,1)} %get-tuple-element.119), channel_id=1, source_target_pairs={{0,8},{8,0},{16,24},{24,16},{1,9},{9,1},{17,25},{25,17},{2,10},{10... | collective-permute-start | bytes 6291464 | tf_op jit(solution)/shard_map/ppermute | solution.py:118
  766.9 106.5 %collective-permute-start.41 = (f32[2560]{0:T(1024)S(1)}, f32[2560]{0:T(1024)S(1)}, u32[]{:S(2)}, u32[]{:S(2)}) collective-permute-start(f32[2560]{0:T(1024)S(1)} %pad_maximum_fusion.71), channel_id=1, source_target_pairs={{0,1},{1,0},{2,3},{3,2},{4,5},{5,4},{6,7},{7,6},{8,9},{9,8},{10,11... | collective-permute-start | bytes 30728 | tf_op jit(solution)/shard_map/ppermute | solution.py:33
  786.2 82.9 %collective-permute-start.52 = (bf16[1024,1024]{1,0:T(8,128)(2,1)}, bf16[1024,1024]{1,0:T(8,128)(2,1)S(1)}, u32[]{:S(2)}, u32[]{:S(2)}) collective-permute-start(bf16[1024,1024]{1,0:T(8,128)(2,1)} %get-tuple-element.121), channel_id=1, source_target_pairs={{0,8},{8,0},{16,24},{24,16},{1,9},{9,1},{17,25},{25,17},{2,10},{10... | collective-permute-start | bytes 6291464 | tf_op jit(solution)/shard_map/ppermute | solution.py:118
  824.9 136.8 %collective-permute-start.39 = (bf16[256,1024]{1,0:T(8,128)(2,1)}, bf16[256,1024]{1,0:T(8,128)(2,1)S(1)}, u32[]{:S(2)}, u32[]{:S(2)}) collective-permute-start(bf16[256,1024]{1,0:T(8,128)(2,1)} %get-tuple-element.69), channel_id=1, source_target_pairs={{0,1},{1,5},{2,3},{3,7},{4,0},{5,4},{6,2},{7,6},{8,9},{9,13},{10,1... | collective-permute-start | bytes 1572872 | tf_op jit(solution)/shard_map/ppermute | solution.py:33
  825.4 136.3 %collective-permute-start.40 = (bf16[256,1024]{1,0:T(8,128)(2,1)S(1)}, bf16[256,1024]{1,0:T(8,128)(2,1)}, u32[]{:S(2)}, u32[]{:S(2)}) collective-permute-start(bf16[256,1024]{1,0:T(8,128)(2,1)S(1)} %get-tuple-element.68), channel_id=1, source_target_pairs={{1,4},{3,6},{4,1},{6,3},{9,12},{11,14},{12,9},{14,11},{17,20},{19,... | collective-permute-start | bytes 1572872 | tf_op jit(solution)/shard_map/ppermute | solution.py:33
  830.5 133.3 %collective-permute-start.63 = (bf16[1024,1024]{1,0:T(8,128)(2,1)S(1)}, bf16[1024,1024]{1,0:T(8,128)(2,1)}, u32[]{:S(2)}, u32[]{:S(2)}) collective-permute-start(bf16[1024,1024]{1,0:T(8,128)(2,1)S(1)} %add_convert_fusion.1), channel_id=1, source_target_pairs={{8,16},{16,8},{9,17},{17,9},{10,18},{18,10},{11,19},{19,11},{12,20... | collective-permute-start | bytes 6291464 | tf_op jit(solution)/shard_map/ppermute | solution.py:125
  871.5 95.0 %collective-permute-start.53 = (bf16[1024,1024]{1,0:T(8,128)(2,1)}, bf16[1024,1024]{1,0:T(8,128)(2,1)}, u32[]{:S(2)}, u32[]{:S(2)}) collective-permute-start(bf16[1024,1024]{1,0:T(8,128)(2,1)} %add_convert_fusion.10), channel_id=1, source_target_pairs={{8,16},{16,8},{9,17},{17,9},{10,18},{18,10},{11,19},{19,11},{12,20... | collective-permute-start | bytes 6291464 | tf_op jit(solution)/shard_map/ppermute | solution.py:125
  969.8 87.6 %collective-permute-start.54 = (bf16[1024,1024]{1,0:T(8,128)(2,1)S(1)}, bf16[1024,1024]{1,0:T(8,128)(2,1)S(1)}, u32[]{:S(2)}, u32[]{:S(2)}) collective-permute-start(bf16[1024,1024]{1,0:T(8,128)(2,1)S(1)} %add_convert_fusion.9), channel_id=1, source_target_pairs={{0,8},{8,0},{16,24},{24,16},{1,9},{9,1},{17,25},{25,17},{2,10},{10... | collective-permute-start | bytes 6291464 | tf_op jit(solution)/shard_map/ppermute | solution.py:118
  (191 other events, 3602.6 us)

commit v2 on v1

v2 whole, which is shorter than its diff:
```python
import jax
import jax.numpy as jnp
from jax import lax
from jax.sharding import PartitionSpec as P

LEN = 1024
EPS = 1e-05
ROTARY_BASE = 10000.0
BF = jnp.bfloat16
F32 = jnp.float32
RC = ("row", "col")


def grid_perm(target):
    pairs = []
    for row in range(4):
        for col in range(2):
            place = target(row // 2, row % 2, col)
            if place is not None:
                pairs.append((row * 2 + col, (place[0] * 2 + place[1]) * 2 + place[2]))
    return pairs


TO_COL = grid_perm(lambda x, k, y: (x, k, 1 - y))
TO_X = grid_perm(lambda x, k, y: (1 - x, k, y))
TO_CORE = grid_perm(lambda x, k, y: (x, 1 - k, y))
SEQ_IN = grid_perm(lambda x, k, y: (1 - x, k, y) if x == y else (x, k, 1 - y))
SEQ_OUT = grid_perm(lambda x, k, y: (x, k, 1 - y) if x == y else (1 - x, k, y))
CROSS = grid_perm(lambda x, k, y: (1 - x, k, 1 - y) if x != y else None)


class Line:
    def __init__(self):
        self.token = lax.create_token()

    def take(self, *values):
        *held, self.token = lax.optimization_barrier(values + (self.token,))
        return held[0] if len(held) == 1 else tuple(held)

    def step(self, work, *inputs):
        held = self.take(*inputs)
        results = work(*held) if len(inputs) > 1 else work(held)
        return self.take(*results) if isinstance(results, tuple) else self.take(results)


def move(value, pairs):
    return lax.ppermute(value, RC, pairs)


def dot(left, right):
    return jnp.dot(left, right, preferred_element_type=F32)


def contract_rows(left, right):
    return lax.dot_general(left, right, (((0,), (0,)), ((), ())), preferred_element_type=F32)


def contract_cols(left, right):
    return lax.dot_general(left, right, (((1,), (1,)), ((), ())), preferred_element_type=F32)


def normalize(rows):
    average = jnp.mean(rows, 1, keepdims=True)
    centred = rows - average
    variance = jnp.mean(centred * centred, 1, keepdims=True)
    inverse = lax.rsqrt(variance + EPS)
    return centred * inverse, inverse


def norm_back(grad_rows, normed, inverse, gain):
    scaled = grad_rows * gain
    grad_in = inverse * (
        scaled
        - jnp.mean(scaled, 1, keepdims=True)
        - normed * jnp.mean(scaled * normed, 1, keepdims=True)
    )
    return grad_in, jnp.sum(grad_rows * normed, 0)


def rotate(values, cosine, sine):
    half = values.shape[1] // 2
    front, back = values[:, :half], values[:, half:]
    return jnp.concatenate((front * cosine - back * sine, front * sine + back * cosine), 1)


def rotate_back(values, cosine, sine):
    half = values.shape[1] // 2
    front, back = values[:, :half], values[:, half:]
    return jnp.concatenate((front * cosine + back * sine, back * cosine - front * sine), 1)


OUTER = [(0, 1), (1, 0), (2, 3), (3, 2)]
INNER = [(1, 2), (2, 1)]
LAG = 3


class ReplicaTotals:
    def __init__(self, line, count):
        self.line = line
        self.count = count
        self.four = lax.axis_size("dp") == 4
        place = lax.axis_index("dp")
        self.outer = (place == 0) | (place == 3)
        self.mine, self.far, self.parts, self.got = [], [], [], []
        self.local, self.other, self.totals, self.finals = [], [], [], []

    def start(self, tile, *inputs):
        far, mine = self.line.step(lambda *held: tile(*held), *inputs)
        self.far.append(move(far, TO_COL))
        self.mine.append(mine)

    def turn(self, index):
        if not self.four:
            if index < self.count:
                part = self.line.step(
                    lambda mine, far: (mine.astype(F32) + far.astype(F32)).astype(BF),
                    self.mine[index],
                    self.far[index],
                )
                self.finals.append(lax.psum(part, "dp").astype(F32))
            return
        count = self.count
        back = index - LAG
        if index < count:
            if back >= 0:
                def join(mine, far, total):
                    part = (mine.astype(F32) + far.astype(F32)).astype(BF)
                    return part, jnp.where(self.outer, part, total)

                part, sent = self.line.step(
                    join, self.mine[index], self.far[index], self.totals[back]
                )
            else:
                part = self.line.step(
                    lambda mine, far: (mine.astype(F32) + far.astype(F32)).astype(BF),
                    self.mine[index],
                    self.far[index],
                )
                sent = part
            self.parts.append(part)
            self.got.append(lax.ppermute(sent, "dp", OUTER))
        elif index < count + LAG:
            self.got.append(lax.ppermute(self.totals[back], "dp", OUTER))

        before = index - 1
        if 0 <= before < count:
            local = self.line.step(
                lambda part, got: (part.astype(F32) + got.astype(F32)).astype(BF),
                self.parts[before],
                self.got[before],
            )
            self.local.append(local)
            self.other.append(lax.ppermute(local, "dp", INNER))
        earlier = index - 2
        if 0 <= earlier < count:
            self.totals.append(
                self.line.step(
                    lambda local, other: (local.astype(F32) + other.astype(F32)).astype(BF),
                    self.local[earlier],
                    self.other[earlier],
                )
            )
        ready = before - LAG
        if 0 <= ready < count:
            self.finals.append(
                self.line.step(
                    lambda got, total: jnp.where(self.outer, got, total).astype(F32),
                    self.got[before],
                    self.totals[ready],
                )
            )


def body(
    tokens,
    grad_out,
    first_gain,
    query_weight,
    key_weight,
    value_weight,
    swish_weight,
    group_gain,
    output_weight,
    second_gain,
    gate_weight,
    up_weight,
    down_weight,
    decay_rate,
):
    row = lax.axis_index("row")
    y = lax.axis_index("col")
    place = lax.axis_index("dp")
    x, k = row // 2, row % 2
    parity = place % 2
    same = x == y
    rows_dev, width = tokens.shape
    quarter = rows_dev // 2

    def sequence_rows(block, got, cross):
        mine = jnp.where(same, block, got)
        other = jnp.where(same, got, cross)
        both = jnp.concatenate((mine, other), 1)
        return jnp.concatenate(
            (
                lax.dynamic_slice_in_dim(both, x * quarter, quarter, 0),
                lax.dynamic_slice_in_dim(both, (1 - x) * quarter, quarter, 0),
            ),
            0,
        )

    def home(rows):
        mine, other = rows[:, :width], rows[:, width:]
        got = move(jnp.where(same, other, mine).astype(BF), SEQ_OUT)
        cross = move(other.astype(BF), CROSS)
        here = jnp.where(same, mine, got.astype(rows.dtype))
        there = jnp.where(same, got, cross).astype(rows.dtype)
        return jnp.where(
            x == 0, jnp.concatenate((here, there), 0), jnp.concatenate((there, here), 0)
        )

    head_values = group_gain.shape[0]
    small = jnp.concatenate((first_gain, second_gain, group_gain, decay_rate))
    small_other = move(small, TO_COL)
    line = Line()
    step, take = line.step, line.take

    count = lax.axis_size("dp")
    even = parity == 0
    swap = [(i, i ^ 1) for i in range(count)]

    def send_half(block):
        half = block.shape[0] // 2
        return lax.dynamic_slice_in_dim(block, parity * half, half, 0)

    def join_halves(first, second):
        return jnp.concatenate(
            (jnp.where(even, first, second), jnp.where(even, second, first)), 0
        )

    def over_dp(value):
        return lax.ppermute(value, "dp", swap)

    def over_col(value):
        return move(value, TO_COL)

    base = 2 * k + x
    block_ids = jnp.bitwise_xor(base, jnp.arange(4, dtype=jnp.int32))
    positions = (
        block_ids[:, None] * quarter + jnp.arange(quarter, dtype=jnp.int32)[None, :]
    ).reshape(-1)
    key_size = query_weight.shape[1] // 2
    value_size = value_weight.shape[1] // 2
    half_key = key_size // 2
    frequency = ROTARY_BASE ** (-jnp.arange(half_key, dtype=F32) / half_key)
    rotation = positions.astype(F32)[:, None] * frequency[None, :]
    distance = positions[:, None] - positions[None, :]
    lag = jnp.maximum(distance, 0).astype(F32)
    head_cols = query_weight.shape[1]
    values = [slice(head * value_size, (head + 1) * value_size) for head in range(2)]

    token_seq, token_cross = move(tokens, SEQ_IN), move(tokens, CROSS)
    query_key_half = over_col(
        step(lambda q, w: send_half(jnp.concatenate((q, w), 1)), query_weight, key_weight)
    )
    cosine, sine = step(lambda turns: (jnp.cos(turns), jnp.sin(turns)), rotation)

    def first_norm(block, got, cross, other_small):
        gain = jnp.concatenate((first_gain, other_small[:width]))
        rows = sequence_rows(block, got, cross).astype(F32)
        normed, inverse = normalize(rows)
        return (normed * gain).astype(BF), rows[:quarter]

    value_half = over_col(step(send_half, value_weight))
    first_half, own_input = step(first_norm, tokens, token_seq, token_cross, small_other)
    first_core = move(first_half, TO_CORE)
    swish_half = over_col(step(send_half, swish_weight))
    second_gain_full = jnp.concatenate((second_gain, small_other[width : 2 * width]))
    first_gain_full = jnp.concatenate((first_gain, small_other[:width]))
    own_group = (group_gain, small_other[2 * width : 2 * width + head_values])
    own_rate = (decay_rate[0], small_other[2 * width + head_values])
    group_gains = tuple(jnp.where(y == 0, own_group[i], own_group[1 - i]) for i in range(2))
    rates = tuple(jnp.where(y == 0, own_rate[i], own_rate[1 - i]) for i in range(2))

    query_key_half = take(query_key_half)
    query_key_swap = over_dp(query_key_half)

    def mine_first(half, core):
        full = jnp.concatenate((half, core), 0)
        rows = full[:, :width]
        return (
            full,
            dot(rows, query_weight),
            dot(rows, key_weight),
            dot(rows, value_weight),
            dot(rows, swish_weight),
        )

    first_in, query_mine, key_mine, value_mine, swish_mine = step(mine_first, first_half, first_core)
    output_send = step(send_half, output_weight)
    value_half = take(value_half)
    value_swap = over_dp(value_half)
    output_half = over_col(output_send)

    masks = step(
        lambda far, near: tuple(
            jnp.where(near >= 0, jnp.exp(-rate * far), 0.0) for rate in rates
        ),
        lag,
        distance,
    )

    def other_query_key(rows, half, swapped, query, key, cos, sin):
        other = join_halves(half, swapped)
        rows = rows[:, width:]
        query = query + dot(rows, other[:, :head_cols])
        key = key + dot(rows, other[:, head_cols:])
        out = [other]
        for head in range(2):
            cut = slice(head * key_size, (head + 1) * key_size)
            out.append(rotate(query[:, cut], cos, sin).astype(BF))
            out.append(rotate(key[:, cut], cos, sin).astype(BF))
        return tuple(out)

    query_key_other, *turned = step(
        other_query_key, first_in, query_key_half, query_key_swap, query_mine, key_mine, cosine, sine
    )
    query_rot, key_rot = turned[::2], turned[1::2]
    query_other, key_other = query_key_other[:, :head_cols], query_key_other[:, head_cols:]

    scores = [
        step(
            lambda q, w, m: (contract_cols(q, w) * m).astype(BF),
            query_rot[head],
            key_rot[head],
            masks[head],
        )
        for head in range(2)
    ]
    swish_half = take(swish_half)
    swish_swap = over_dp(swish_half)

    def other_value(rows, half, swapped, value):
        other = join_halves(half, swapped)
        return other, (value + dot(rows[:, width:], other)).astype(BF)

    value_other, valued = step(other_value, first_in, value_half, value_swap, value_mine)
    grad_held = take(grad_out)
    grad_seq, grad_cross = move(grad_held, SEQ_IN), move(grad_held, CROSS)

    def retain(weighted, value):
        retained = dot(weighted, value)
        average = jnp.mean(retained, 1, keepdims=True)
        centred = retained - average
        variance = jnp.mean(centred * centred, 1, keepdims=True)
        inverse = lax.rsqrt(jnp.maximum(variance, 1.0))
        return centred * inverse, inverse, (variance > 1.0).astype(F32)

    retained = [step(retain, scores[0], valued[:, values[0]])]
    output_half = take(output_half)
    output_swap = over_dp(output_half)
    gate_half = over_col(step(send_half, gate_weight))
    retained.append(step(retain, scores[1], valued[:, values[1]]))

    def gating(rows, half, swapped, swish, first_normed, second_normed, gain0, gain1):
        other = join_halves(half, swapped)
        swish = swish + dot(rows[:, width:], other)
        gate = jax.nn.silu(swish)
        gated = jnp.concatenate(
            (
                gate[:, values[0]] * first_normed * gain0,
                gate[:, values[1]] * second_normed * gain1,
            ),
            1,
        )
        return other, swish, gated.astype(BF)

    swish_other, swish_in, gated = step(
        gating,
        first_in,
        swish_half,
        swish_swap,
        swish_mine,
        retained[0][0],
        retained[1][0],
        *group_gains,
    )
    up_half = over_col(step(send_half, up_weight))
    grad_half = step(sequence_rows, grad_out, grad_seq, grad_cross)
    grad_core = move(grad_half, TO_CORE)

    half_rows = 2 * quarter

    def project(rows, mine, other):
        return dot(rows, mine), dot(rows, other)

    def project_scatter(rows, mine, other):
        back = step(
            lambda r, m, o: jnp.concatenate(
                (dot(r, m).astype(BF), dot(r, o).astype(BF)), 1
            ),
            rows[half_rows:],
            mine,
            other,
        )
        from_core = move(back, TO_CORE)
        front = step(
            lambda r, m, o: jnp.concatenate((dot(r, m), dot(r, o)), 1), rows[:half_rows], mine, other
        )
        return reduce_row(front, from_core)

    def reduce_row(front, from_core):
        def add(part, core):
            both = part + core.astype(F32)
            return both[:quarter], both[quarter:].astype(BF)

        own, away = step(add, front, from_core)
        return own, move(away, TO_X)

    output_other = step(join_halves, output_half, output_swap)
    gate_half = take(gate_half)
    gate_swap = over_dp(gate_half)
    own_out, out_x = project_scatter(gated, output_weight, output_other)
    grad_rows = step(lambda a, b: jnp.concatenate((a, b), 0), grad_half, grad_core)
    down_half = over_col(step(send_half, down_weight))

    def second_norm(rows, own, away, gain):
        mid = rows + own + away.astype(F32)
        normed, inverse = normalize(mid)
        return mid, normed, inverse, (normed * gain).astype(BF)

    x_mid, second_normed, second_inv, second_own = step(
        second_norm, own_input, own_out, out_x, second_gain_full
    )

    def gather_start(own):
        return move(own, TO_X), move(own, TO_CORE)

    second_x, second_core = gather_start(second_own)
    up_half = take(up_half)
    up_swap = over_dp(up_half)
    gate_other = step(join_halves, gate_half, gate_swap)
    second_x = take(second_x)
    second_both = move(second_x, TO_CORE)
    up_other = step(join_halves, up_half, up_swap)
    down_half = take(down_half)
    down_swap = over_dp(down_half)

    def feed(own, from_x, core, both, gate_o, up_o):
        rows = jnp.concatenate((own, from_x, core, both), 0)
        near, far = rows[:, :width], rows[:, width:]
        gate_pre = dot(near, gate_weight) + dot(far, gate_o)
        up_pre = dot(near, up_weight) + dot(far, up_o)
        return rows, gate_pre, up_pre, (jax.nn.gelu(gate_pre) * up_pre).astype(BF)

    second_in, gate_pre, up_pre, hidden = step(
        feed, second_own, second_x, second_core, second_both, gate_other, up_other
    )

    totals = ReplicaTotals(line, 14)
    tile_rows = width // 2

    def tile_in(piece):
        def tile(left, right):
            near = left[:, piece * tile_rows : (piece + 1) * tile_rows]
            far = left[:, width + piece * tile_rows : width + (piece + 1) * tile_rows]
            return contract_rows(far, right).astype(BF), contract_rows(near, right).astype(BF)

        return tile

    def tile_out(piece):
        def tile(left, right):
            left = left[:, piece * tile_rows : (piece + 1) * tile_rows]
            return (
                contract_rows(left, right[:, width:]).astype(BF),
                contract_rows(left, right[:, :width]).astype(BF),
            )

        return tile

    totals.start(tile_out(0), hidden, grad_rows)
    totals.start(tile_out(1), hidden, grad_rows)
    down_other = step(join_halves, down_half, down_swap)

    def feed_back(grads, gate, up, down_o):
        grad_hidden = contract_cols(grads[:, :width], down_weight) + contract_cols(
            grads[:, width:], down_o
        )
        value, pull = jax.vjp(jax.nn.gelu, gate)
        return pull(grad_hidden * up)[0].astype(BF), (grad_hidden * value).astype(BF)

    grad_gate, grad_up = step(feed_back, grad_rows, gate_pre, up_pre, down_other)

    def back_half(rows, low, terms):
        flat = [value for term in terms for value in term]

        def total(*held):
            out = []
            for side in (1, 2):
                part = None
                for index in range(len(terms)):
                    grad, weight = held[3 * index], held[3 * index + side]
                    value = contract_cols(grad[rows], weight)
                    part = value if part is None else part + value
                out.append(part.astype(BF) if low else part)
            return jnp.concatenate(out, 1)

        return step(total, *flat)

    feed_terms = ((grad_gate, gate_weight, gate_other), (grad_up, up_weight, up_other))
    back = back_half(slice(half_rows, None), True, feed_terms)
    second_from_core = move(back, TO_CORE)
    totals.turn(0)
    totals.start(tile_in(0), second_in, grad_gate)
    front = back_half(slice(0, half_rows), False, feed_terms)
    own_second, second_away = reduce_row(front, second_from_core)
    totals.turn(1)
    totals.start(tile_in(1), second_in, grad_gate)

    def middle(own, away, normed, inverse, gain, own_grad):
        grad_in, gain_part = norm_back(own + away.astype(F32), normed, inverse, gain)
        mid = own_grad.astype(F32) + grad_in
        return mid, mid.astype(BF), gain_part

    grad_mid, attn_own, second_gain_part = step(
        middle, own_second, second_away, second_normed, second_inv, second_gain_full, grad_half[:quarter]
    )
    attn_x, attn_core = gather_start(attn_own)
    totals.turn(2)
    totals.start(tile_in(0), second_in, grad_up)
    attn_x = take(attn_x)
    attn_both = move(attn_x, TO_CORE)
    totals.turn(3)
    totals.start(tile_in(1), second_in, grad_up)

    def gated_back(own, from_x, core, both, output_o):
        rows = jnp.concatenate((own, from_x, core, both), 0)
        return rows, contract_cols(rows[:, :width], output_weight) + contract_cols(
            rows[:, width:], output_o
        )

    attn_in, grad_gated = step(gated_back, attn_own, attn_x, attn_core, attn_both, output_other)
    totals.turn(4)
    totals.start(tile_out(0), gated, attn_in)

    def head_back(grad_head, swish, gain, normed, inverse, open_floor):
        swish_out, pull = jax.vjp(jax.nn.silu, swish)
        gain_part = jnp.sum(grad_head * swish_out * normed, 0)
        product = grad_head * gain
        grad_normed = product * swish_out
        grad_swish = pull(product * normed)[0].astype(BF)
        grad_retained = (
            inverse
            * (
                grad_normed
                - jnp.mean(grad_normed, 1, keepdims=True)
                - open_floor * normed * jnp.mean(grad_normed * normed, 1, keepdims=True)
            )
        ).astype(BF)
        return gain_part, grad_swish, grad_retained

    heads = [
        step(
            head_back,
            grad_gated[:, values[head]],
            swish_in[:, values[head]],
            group_gains[head],
            *retained[head],
        )
        for head in range(2)
    ]
    group_gain_parts = [head[0] for head in heads]
    grad_swish = step(lambda a, b: jnp.concatenate((a, b), 1), heads[0][1], heads[1][1])
    totals.turn(5)
    totals.start(tile_out(1), gated, attn_in)

    def retain_back(grad, weighted, value, mask, q, w, cos, sin):
        grad_value = contract_rows(weighted, grad).astype(BF)
        grad_scores = (contract_cols(grad, value) * mask).astype(BF)
        return (
            grad_value,
            rotate_back(dot(grad_scores, w), cos, sin).astype(BF),
            rotate_back(contract_rows(grad_scores, q), cos, sin).astype(BF),
        )

    backs = []
    for head in range(2):
        backs.append(
            step(
                retain_back,
                heads[head][2],
                scores[head],
                valued[:, values[head]],
                masks[head],
                query_rot[head],
                key_rot[head],
                cosine,
                sine,
            )
        )
        totals.turn(6 + head)
        totals.start(tile_in(head), first_in, grad_swish)
    grad_value, grad_query, grad_key, grad_query_key = step(
        lambda v0, q0, k0, v1, q1, k1: (
            jnp.concatenate((v0, v1), 1),
            jnp.concatenate((q0, q1), 1),
            jnp.concatenate((k0, k1), 1),
            jnp.concatenate((q0, q1, k0, k1), 1),
        ),
        *backs[0],
        *backs[1],
    )
    head_terms = (
        (grad_query, query_weight, query_other),
        (grad_key, key_weight, key_other),
        (grad_value, value_weight, value_other),
        (grad_swish, swish_weight, swish_other),
    )
    back = back_half(slice(half_rows, None), True, head_terms)
    first_from_core = move(back, TO_CORE)
    totals.turn(8)
    totals.start(tile_in(0), first_in, grad_value)
    front = back_half(slice(0, half_rows), False, head_terms)
    own_first, first_away = reduce_row(front, first_from_core)
    totals.turn(9)
    totals.start(tile_in(1), first_in, grad_value)

    def last(own, away, rows, gain, mid):
        normed, inverse = normalize(rows)
        grad_in, gain_part = norm_back(own + away.astype(F32), normed, inverse, gain)
        return mid + grad_in, gain_part

    input_own, first_gain_part = step(
        last, own_first, first_away, own_input, first_gain_full, grad_mid
    )
    totals.turn(10)
    totals.start(tile_in(0), first_in, grad_query_key)
    input_grad = home(input_own)
    totals.turn(11)
    totals.start(tile_in(1), first_in, grad_query_key)
    own_down, down_away = project_scatter(hidden, down_weight, down_other)
    totals.turn(12)
    block_own = step(
        lambda mid, own, away: (mid + own + away.astype(F32)).astype(BF), x_mid, own_down, down_away
    )
    block_out = home(block_own)
    totals.turn(13)
    for index in range(14, 14 + LAG + 1):
        totals.turn(index)
    finals = totals.finals
    down_grad, gate_grad, up_grad, output_grad, swish_grad, value_grad, query_key_grad = (
        jnp.concatenate((finals[2 * i], finals[2 * i + 1]), 0) for i in range(7)
    )
    query_grad, key_grad = query_key_grad[:, :head_cols], query_key_grad[:, head_cols:]

    group_pair = jnp.where(
        y == 0,
        jnp.stack(group_gain_parts),
        jnp.stack(group_gain_parts[::-1]),
    )
    outgoing = jnp.concatenate((first_gain_part[width:], second_gain_part[width:], group_pair[1]))
    incoming = move(outgoing, TO_COL)
    gains = jnp.concatenate((first_gain_part[:width], second_gain_part[:width])) + incoming[: 2 * width]
    gains = gains + move(gains, TO_CORE)
    gains = gains + move(gains, TO_X)
    gains = jnp.concatenate((gains, group_pair[0] + incoming[2 * width :]))
    if lax.axis_size("dp") == 4:
        gains = gains + lax.ppermute(gains, "dp", OUTER)
        gains = gains + lax.ppermute(gains, "dp", [(0, 3), (3, 0), (1, 2), (2, 1)])
    else:
        gains = lax.psum(gains, "dp")
    group_gain_grad = gains[2 * width :]
    return (
        block_out,
        input_grad,
        gains[:width],
        query_grad,
        key_grad,
        value_grad,
        swish_grad,
        group_gain_grad,
        output_grad,
        gains[width : 2 * width],
        gate_grad,
        up_grad,
        down_grad,
    )


def solution(mesh):
    placed = (
        P(("dp", "row"), "col"),
        P(("dp", "row"), "col"),
        P("col"),
        P("col", "row"),
        P("col", "row"),
        P("col", "row"),
        P("col", "row"),
        P(("row", "col")),
        P("row", "col"),
        P("col"),
        P("col", "row"),
        P("col", "row"),
        P("row", "col"),
        P(("row", "col")),
    )
    return jax.shard_map(
        body,
        mesh=mesh,
        in_specs=placed,
        out_specs=(
            P(("dp", "row"), "col"),
            P(("dp", "row"), "col"),
            P("col"),
            P("col", "row"),
            P("col", "row"),
            P("col", "row"),
            P("col", "row"),
            P(("row", "col")),
            P("row", "col"),
            P("col"),
            P("col", "row"),
            P("col", "row"),
            P("row", "col"),
        ),
        check_vma=False,
    )
```

time: 1070 us -> 845 us (0.79)
  waiting for transfers between devices: 470 us -> 288 us
  blocking collectives: 86.9 us -> 0 us
  matrix products: 192 us -> 154 us
  local copies, waits for them, and re-layouts: 38.1 us -> 67.1 us
  other arithmetic: 120 us -> 147 us
  starting transfers between devices: 148 us -> 172 us
    ppermute x41 -> x49, waiting for transfers between devices: 244 us -> 150 us  [move(): return lax.ppermute(value, RC, pairs)]
    ppermute x24 -> x40, waiting for transfers between devices: 225 us -> 138 us  [the longest x14 91.8 us: turn(): self.got.append(lax.ppermute(sent, 'dp', OUTER))]
    psum x1 -> x0, blocking collectives: 86.9 us -> none  [body(): gains = lax.psum(jnp.concatenate((gains, placed)), ('dp', 'row'))]
    dot_general x18 -> x32, matrix products: 71.1 us -> 49.7 us  [contract_rows(): lax.dot_general(left, right, (((0,), (0,)), ((), ())), preferred_element_...]
    concatenate x10 -> x32, other arithmetic: 11.1 us -> 30 us  [the longest x6 15 us: body(): jnp.concatenate((finals[2 * i], finals[2 * i + 1]), 0)]
    select_n x8 -> x20, other arithmetic: 12.3 us -> 31 us  [the longest x11 16.6 us: join(): return (part, jnp.where(self.outer, part, total))]
    ppermute x41 -> x49, starting transfers between devices: 44.8 us -> 62.5 us  [move(): return lax.ppermute(value, RC, pairs)]
    unnamed x9 -> x1, other arithmetic: 15.8 us -> 0.07 us
  transfers between devices with their start and end apart: 65 -> 89, of which waited for: 24 -> 32; matrix products, arithmetic and copies ran while one was open for 24% -> 38% of each run, Pallas kernels for 0% -> 0%
where the time goes in v2:
time: 845 us; the launch traced here: 833 us
  waiting for transfers between devices  288 us (34%)
  starting transfers between devices  172 us (20%)
  matrix products  154 us (18%)
  other arithmetic  147 us (17%)
  local copies, waits for them, and re-layouts  67.1 us (8%)
    ppermute x49, waiting for transfers between devices, move(): return lax.ppermute(value, RC, pairs)  150 us
    ppermute x14, waiting for transfers between devices, turn(): self.got.append(lax.ppermute(sent, 'dp', OUTER))  91.8 us
    ppermute x49, starting transfers between devices, move(): return lax.ppermute(value, RC, pairs)  62.5 us
    ppermute x14, starting transfers between devices, turn(): self.got.append(lax.ppermute(sent, 'dp', OUTER))  57.5 us
    dot_general x24, matrix products, dot(): return jnp.dot(left, right, preferred_element_type=F32)  52.3 us
    dot_general x32, matrix products, contract_cols(): lax.dot_general(left, right, (((1,), (1,)), ((), ())), preferred_element_...  51.9 us
    dot_general x32, matrix products, contract_rows(): lax.dot_general(left, right, (((0,), (0,)), ((), ())), preferred_element_...  49.7 us
    unnamed x247, local copies, waits for them, and re-layouts  36.6 us
  transfers between devices with their start and end apart: 89, of which 32 were waited for; matrix products, arithmetic and copies ran while one was open for 38% of the time, Pallas kernels for 0%

profile of v2, /device:TPU:0, one launch (start us, length us, event | category | flops | bytes accessed | tf_op | source)
XLA Modules:
  0.0 833.5 jit_solution(317385444113327757)
XLA Ops:
  15.7 11.6 %collective-permute-done.2 = f32[2561]{0:T(1024)S(1)} collective-permute-done((f32[2561]{0:T(1024)S(1)}, f32[2561]{0:T(1024)S(1)}, u32[]{:S(2)}, u32[]{:S(2)}) %collective-permute-start.2) | collective-permute-done | bytes 10276 | tf_op jit(solution)/shard_map/ppermute | solution.py:47
  48.0 16.1 %collective-permute-done.4 = bf16[512,1024]{1,0:T(8,128)(2,1)} collective-permute-done((bf16[512,1024]{1,0:T(8,128)(2,1)}, bf16[512,1024]{1,0:T(8,128)(2,1)}, u32[]{:S(2)}, u32[]{:S(2)}) %collective-permute-start.4) | collective-permute-done | bytes 1048608 | tf_op jit(solution)/shard_map/ppermute | solution.py:47
  110.8 9.9 %collective-permute-done.9 = bf16[512,1024]{1,0:T(8,128)(2,1)S(1)} collective-permute-done((bf16[512,1024]{1,0:T(8,128)(2,1)}, bf16[512,1024]{1,0:T(8,128)(2,1)S(1)}, u32[]{:S(2)}, u32[]{:S(2)}) %collective-permute-start.9) | collective-permute-done | bytes 1048608 | tf_op jit(solution)/shard_map/ppermute | solution.py:241
  142.7 10.3 %collective-permute-done.10 = bf16[512,1024]{1,0:T(8,128)(2,1)} collective-permute-done((bf16[512,1024]{1,0:T(8,128)(2,1)}, bf16[512,1024]{1,0:T(8,128)(2,1)}, u32[]{:S(2)}, u32[]{:S(2)}) %collective-permute-start.10) | collective-permute-done | bytes 1048608 | tf_op jit(solution)/shard_map/ppermute | solution.py:47
  207.2 18.0 %collective-permute-done.16 = bf16[256,2048]{1,0:T(8,128)(2,1)S(1)} collective-permute-done((bf16[256,2048]{1,0:T(8,128)(2,1)S(1)}, bf16[256,2048]{1,0:T(8,128)(2,1)S(1)}, u32[]{:S(2)}, u32[]{:S(2)}) %collective-permute-start.16) | collective-permute-done | bytes 1048608 | tf_op jit(solution)/shard_map/ppermute | solution.py:47
  233.2 19.3 %collective-permute-done.18 = bf16[256,2048]{1,0:T(8,128)(2,1)} collective-permute-done((bf16[256,2048]{1,0:T(8,128)(2,1)S(1)}, bf16[256,2048]{1,0:T(8,128)(2,1)}, u32[]{:S(2)}, u32[]{:S(2)}) %collective-permute-start.18) | collective-permute-done | bytes 1048608 | tf_op jit(solution)/shard_map/ppermute | solution.py:47
  270.9 8.2 fusion.15
  294.1 8.6 %multiply_convert_fusion.2 = (bf16[1024,1024]{1,0:T(8,128)(2,1)S(1)}, bf16[1024,1024]{1,0:T(8,128)(2,1)S(1)}) fusion(f32[1024,1024]{1,0:T(8,128)} %copy-done.118, f32[1024,1024]{1,0:T(8,128)} %get-tuple-element.999, f32[1024,1024]{1,0:T(8,128)} %fusion.40, bf16[1024,1024]{1,0:T(8,128)(2,1)S(1)} %copy-done, bf16[1024,2048]{1,0:T(8,128)(2,1)S(1)} %copy-done.45), kind=kOutput, calls=%fused_computation.35 | convolution fusion | flops 2173698048 | bytes 20971520 | tf_op jit(solution)/shard_map/dot_general | solution.py:59
  311.2 23.6 %collective-permute-done.26 = bf16[512,1024]{1,0:T(8,128)(2,1)} collective-permute-done((bf16[512,1024]{1,0:T(8,128)(2,1)}, bf16[512,1024]{1,0:T(8,128)(2,1)}, u32[]{:S(2)}, u32[]{:S(2)}) %collective-permute-start.26) | collective-permute-done | bytes 1048608 | tf_op jit(solution)/shard_map/ppermute | solution.py:47
  352.9 12.9 %collective-permute-done.29 = bf16[512,1024]{1,0:T(8,128)(2,1)} collective-permute-done((bf16[512,1024]{1,0:T(8,128)(2,1)S(1)}, bf16[512,1024]{1,0:T(8,128)(2,1)}, u32[]{:S(2)}, u32[]{:S(2)}) %collective-permute-start.29) | collective-permute-done | bytes 1048608 | tf_op jit(solution)/shard_map/ppermute | solution.py:141
  380.0 16.4 %collective-permute-done.33 = bf16[512,1024]{1,0:T(8,128)(2,1)S(1)} collective-permute-done((bf16[512,1024]{1,0:T(8,128)(2,1)S(1)}, bf16[512,1024]{1,0:T(8,128)(2,1)S(1)}, u32[]{:S(2)}, u32[]{:S(2)}) %collective-permute-start.33) | collective-permute-done | bytes 1048608 | tf_op jit(solution)/shard_map/ppermute | solution.py:141
  406.2 12.8 %collective-permute-done.31 = bf16[256,2048]{1,0:T(8,128)(2,1)S(1)} collective-permute-done((bf16[256,2048]{1,0:T(8,128)(2,1)S(1)}, bf16[256,2048]{1,0:T(8,128)(2,1)S(1)}, u32[]{:S(2)}, u32[]{:S(2)}) %collective-permute-start.31) | collective-permute-done | bytes 1048608 | tf_op jit(solution)/shard_map/ppermute | solution.py:47
  445.9 10.7 %collective-permute-done.40 = bf16[512,1024]{1,0:T(8,128)(2,1)S(1)} collective-permute-done((bf16[512,1024]{1,0:T(8,128)(2,1)S(1)}, bf16[512,1024]{1,0:T(8,128)(2,1)S(1)}, u32[]{:S(2)}, u32[]{:S(2)}) %collective-permute-start.40) | collective-permute-done | bytes 1048608 | tf_op jit(solution)/shard_map/ppermute | solution.py:141
  476.0 15.8 %collective-permute-done.43 = bf16[512,1024]{1,0:T(8,128)(2,1)S(1)} collective-permute-done((bf16[512,1024]{1,0:T(8,128)(2,1)S(1)}, bf16[512,1024]{1,0:T(8,128)(2,1)S(1)}, u32[]{:S(2)}, u32[]{:S(2)}) %collective-permute-start.43) | collective-permute-done | bytes 1048608 | tf_op jit(solution)/shard_map/ppermute | solution.py:141
  543.2 15.4 %collective-permute-start.52 = (bf16[512,1024]{1,0:T(8,128)(2,1)}, bf16[512,1024]{1,0:T(8,128)(2,1)S(1)}, u32[]{:S(2)}, u32[]{:S(2)}) collective-permute-start(bf16[512,1024]{1,0:T(8,128)(2,1)} %get-tuple-element.1292), channel_id=1, source_target_pairs={{0,8},{8,0},{16,24},{24,16},{1,9},{9,1},{17,25},{25,17},{2,10},{10... | collective-permute-start | bytes 3145736 | tf_op jit(solution)/shard_map/ppermute | solution.py:141
  575.4 9.6 %collective-permute-done.54 = bf16[512,1024]{1,0:T(8,128)(2,1)} collective-permute-done((bf16[512,1024]{1,0:T(8,128)(2,1)}, bf16[512,1024]{1,0:T(8,128)(2,1)}, u32[]{:S(2)}, u32[]{:S(2)}) %collective-permute-start.54) | collective-permute-done | bytes 1048608 | tf_op jit(solution)/shard_map/ppermute | solution.py:47
  693.1 8.1 collective-permute-done.70
  705.5 8.2 collective-permute-start.80
  714.7 8.8 %collective-permute-done.67 = bf16[256,2048]{1,0:T(8,128)(2,1)S(1)} collective-permute-done((bf16[256,2048]{1,0:T(8,128)(2,1)S(1)}, bf16[256,2048]{1,0:T(8,128)(2,1)S(1)}, u32[]{:S(2)}, u32[]{:S(2)}) %collective-permute-start.67) | collective-permute-done | bytes 1048608 | tf_op jit(solution)/shard_map/ppermute | solution.py:47
  724.9 11.9 %collective-permute-done.80 = bf16[512,1024]{1,0:T(8,128)(2,1)S(1)} collective-permute-done((bf16[512,1024]{1,0:T(8,128)(2,1)S(1)}, bf16[512,1024]{1,0:T(8,128)(2,1)S(1)}, u32[]{:S(2)}, u32[]{:S(2)}) %collective-permute-start.80) | collective-permute-done | bytes 1048608 | tf_op jit(solution)/shard_map/ppermute | solution.py:141
  749.1 15.8 %collective-permute-done.83 = bf16[512,1024]{1,0:T(8,128)(2,1)S(1)} collective-permute-done((bf16[512,1024]{1,0:T(8,128)(2,1)S(1)}, bf16[512,1024]{1,0:T(8,128)(2,1)S(1)}, u32[]{:S(2)}, u32[]{:S(2)}) %collective-permute-start.83) | collective-permute-done | bytes 1048608 | tf_op jit(solution)/shard_map/ppermute | solution.py:141
  772.8 18.5 %collective-permute-start.88 = (bf16[512,1024]{1,0:T(8,128)(2,1)S(1)}, bf16[512,1024]{1,0:T(8,128)(2,1)S(1)}, u32[]{:S(2)}, u32[]{:S(2)}) collective-permute-start(bf16[512,1024]{1,0:T(8,128)(2,1)S(1)} %add_convert_fusion.1), channel_id=1, source_target_pairs={{0,8},{8,0},{16,24},{24,16},{1,9},{9,1},{17,25},{25,17},{2,10},{10... | collective-permute-start | bytes 3145736 | tf_op jit(solution)/shard_map/ppermute | solution.py:143
  792.9 16.9 %collective-permute-done.85 = bf16[512,1024]{1,0:T(8,128)(2,1)S(1)} collective-permute-done((bf16[512,1024]{1,0:T(8,128)(2,1)S(1)}, bf16[512,1024]{1,0:T(8,128)(2,1)S(1)}, u32[]{:S(2)}, u32[]{:S(2)}) %collective-permute-start.85) | collective-permute-done | bytes 1048608 | tf_op jit(solution)/shard_map/ppermute | solution.py:143
  812.7 17.8 %collective-permute-done.88 = bf16[512,1024]{1,0:T(8,128)(2,1)S(1)} collective-permute-done((bf16[512,1024]{1,0:T(8,128)(2,1)S(1)}, bf16[512,1024]{1,0:T(8,128)(2,1)S(1)}, u32[]{:S(2)}, u32[]{:S(2)}) %collective-permute-start.88) | collective-permute-done | bytes 1048608 | tf_op jit(solution)/shard_map/ppermute | solution.py:143
  (716 shorter events, 502.1 us)
Async XLA Ops:
  39.8 46.8 %collective-permute-start.7 = (bf16[512,1024]{1,0:T(8,128)(2,1)}, bf16[512,1024]{1,0:T(8,128)(2,1)}, u32[]{:S(2)}, u32[]{:S(2)}) collective-permute-start(bf16[512,1024]{1,0:T(8,128)(2,1)} %constant_dynamic-slice_fusion.5), channel_id=1, source_target_pairs={{0,1},{1,0},{2,3},{3,2},{4,5},{5,4},{6,7},{7,6},{8,9},{9,8},{10,11... | collective-permute-start | bytes 3145736 | tf_op jit(solution)/shard_map/ppermute | solution.py:47
  65.8 43.2 %collective-permute-start.5 = (bf16[512,1024]{1,0:T(8,128)(2,1)}, bf16[512,1024]{1,0:T(8,128)(2,1)}, u32[]{:S(2)}, u32[]{:S(2)}) collective-permute-start(bf16[512,1024]{1,0:T(8,128)(2,1)} %constant_dynamic-slice_fusion.4), channel_id=1, source_target_pairs={{0,1},{1,0},{2,3},{3,2},{4,5},{5,4},{6,7},{7,6},{8,9},{9,8},{10,11... | collective-permute-start | bytes 3145736 | tf_op jit(solution)/shard_map/ppermute | solution.py:47
  96.2 56.8 %collective-permute-start.10 = (bf16[512,1024]{1,0:T(8,128)(2,1)}, bf16[512,1024]{1,0:T(8,128)(2,1)}, u32[]{:S(2)}, u32[]{:S(2)}) collective-permute-start(bf16[512,1024]{1,0:T(8,128)(2,1)} %constant_dynamic-slice_fusion.3), channel_id=1, source_target_pairs={{0,1},{1,0},{2,3},{3,2},{4,5},{5,4},{6,7},{7,6},{8,9},{9,8},{10,11... | collective-permute-start | bytes 3145736 | tf_op jit(solution)/shard_map/ppermute | solution.py:47
  109.0 58.1 %collective-permute-start.8 = (bf16[512,1024]{1,0:T(8,128)(2,1)}, bf16[512,1024]{1,0:T(8,128)(2,1)}, u32[]{:S(2)}, u32[]{:S(2)}) collective-permute-start(bf16[512,1024]{1,0:T(8,128)(2,1)} %collective-permute-done.5), channel_id=1, source_target_pairs={{0,8},{8,0},{16,24},{24,16},{1,9},{9,1},{17,25},{25,17},{2,10},{10... | collective-permute-start | bytes 3145736 | tf_op jit(solution)/shard_map/ppermute | solution.py:241
  127.3 56.1 %collective-permute-start.13 = (bf16[512,1024]{1,0:T(8,128)(2,1)}, bf16[512,1024]{1,0:T(8,128)(2,1)}, u32[]{:S(2)}, u32[]{:S(2)}) collective-permute-start(bf16[512,1024]{1,0:T(8,128)(2,1)} %param.15), channel_id=1, source_target_pairs={{1,4},{3,6},{4,1},{6,3},{9,12},{11,14},{12,9},{14,11},{17,20},{19,... | collective-permute-start | bytes 3145736 | tf_op jit(solution)/shard_map/ppermute | solution.py:47
  128.9 54.5 %collective-permute-start.12 = (bf16[512,1024]{1,0:T(8,128)(2,1)}, bf16[512,1024]{1,0:T(8,128)(2,1)}, u32[]{:S(2)}, u32[]{:S(2)}) collective-permute-start(bf16[512,1024]{1,0:T(8,128)(2,1)} %param.15), channel_id=1, source_target_pairs={{0,4},{1,0},{2,6},{3,2},{4,5},{5,1},{6,7},{7,3},{8,12},{9,8},{10,1... | collective-permute-start | bytes 3145736 | tf_op jit(solution)/shard_map/ppermute | solution.py:47
  287.6 62.2 %collective-permute-start.30 = (bf16[512,1024]{1,0:T(8,128)(2,1)}, bf16[512,1024]{1,0:T(8,128)(2,1)}, u32[]{:S(2)}, u32[]{:S(2)}) collective-permute-start(bf16[512,1024]{1,0:T(8,128)(2,1)} %fusion.78), channel_id=1, source_target_pairs={{0,1},{1,0},{2,3},{3,2},{4,5},{5,4},{6,7},{7,6},{8,9},{9,8},{10,11... | collective-permute-start | bytes 3145736 | tf_op jit(solution)/shard_map/ppermute | solution.py:47
  288.2 46.6 %collective-permute-start.26 = (bf16[512,1024]{1,0:T(8,128)(2,1)}, bf16[512,1024]{1,0:T(8,128)(2,1)}, u32[]{:S(2)}, u32[]{:S(2)}) collective-permute-start(bf16[512,1024]{1,0:T(8,128)(2,1)} %fusion.72), channel_id=1, source_target_pairs={{0,1},{1,0},{2,3},{3,2},{4,5},{5,4},{6,7},{7,6},{8,9},{9,8},{10,11... | collective-permute-start | bytes 3145736 | tf_op jit(solution)/shard_map/ppermute | solution.py:47
  308.3 40.2 %collective-permute-start.27 = (bf16[512,2048]{1,0:T(8,128)(2,1)S(1)}, bf16[512,2048]{1,0:T(8,128)(2,1)S(1)}, u32[]{:S(2)}, u32[]{:S(2)}) collective-permute-start(bf16[512,2048]{1,0:T(8,128)(2,1)S(1)} %pad_maximum_fusion.22), channel_id=1, source_target_pairs={{0,2},{1,3},{2,0},{3,1},{4,6},{5,7},{6,4},{7,5},{8,10},{9,11},{10,... | collective-permute-start | bytes 6291464 | tf_op jit(solution)/shard_map/ppermute | solution.py:47
  340.1 38.4 %collective-permute-start.34 = (bf16[512,1024]{1,0:T(8,128)(2,1)}, bf16[512,1024]{1,0:T(8,128)(2,1)}, u32[]{:S(2)}, u32[]{:S(2)}) collective-permute-start(bf16[512,1024]{1,0:T(8,128)(2,1)} %convolution_convert_fusion.23), channel_id=1, source_target_pairs={{0,1},{1,0},{2,3},{3,2},{4,5},{5,4},{6,7},{7,6},{8,9},{9,8},{10,11... | collective-permute-start | bytes 3145736 | tf_op jit(solution)/shard_map/ppermute | solution.py:47
  370.0 50.7 %collective-permute-start.39 = (bf16[512,1024]{1,0:T(8,128)(2,1)S(1)}, bf16[512,1024]{1,0:T(8,128)(2,1)S(1)}, u32[]{:S(2)}, u32[]{:S(2)}) collective-permute-start(bf16[512,1024]{1,0:T(8,128)(2,1)S(1)} %convolution_convert_fusion.21), channel_id=1, source_target_pairs={{0,1},{1,0},{2,3},{3,2},{4,5},{5,4},{6,7},{7,6},{8,9},{9,8},{10,11... | collective-permute-start | bytes 3145736 | tf_op jit(solution)/shard_map/ppermute | solution.py:47
  425.8 49.3 %collective-permute-start.45 = (bf16[512,1024]{1,0:T(8,128)(2,1)S(1)}, bf16[512,1024]{1,0:T(8,128)(2,1)S(1)}, u32[]{:S(2)}, u32[]{:S(2)}) collective-permute-start(bf16[512,1024]{1,0:T(8,128)(2,1)S(1)} %convolution_convert_fusion.17), channel_id=1, source_target_pairs={{0,1},{1,0},{2,3},{3,2},{4,5},{5,4},{6,7},{7,6},{8,9},{9,8},{10,11... | collective-permute-start | bytes 3145736 | tf_op jit(solution)/shard_map/ppermute | solution.py:47
  463.0 41.8 %collective-permute-start.48 = (bf16[512,1024]{1,0:T(8,128)(2,1)S(1)}, bf16[512,1024]{1,0:T(8,128)(2,1)S(1)}, u32[]{:S(2)}, u32[]{:S(2)}) collective-permute-start(bf16[512,1024]{1,0:T(8,128)(2,1)S(1)} %fusion.84), channel_id=1, source_target_pairs={{0,1},{1,0},{2,3},{3,2},{4,5},{5,4},{6,7},{7,6},{8,9},{9,8},{10,11... | collective-permute-start | bytes 3145736 | tf_op jit(solution)/shard_map/ppermute | solution.py:47
  475.9 38.4 %collective-permute-start.46 = (bf16[512,1024]{1,0:T(8,128)(2,1)S(1)}, bf16[512,1024]{1,0:T(8,128)(2,1)S(1)}, u32[]{:S(2)}, u32[]{:S(2)}) collective-permute-start(bf16[512,1024]{1,0:T(8,128)(2,1)S(1)} %get-tuple-element.1215), channel_id=1, source_target_pairs={{0,8},{8,0},{16,24},{24,16},{1,9},{9,1},{17,25},{25,17},{2,10},{10... | collective-permute-start | bytes 3145736 | tf_op jit(solution)/shard_map/ppermute | solution.py:141
  541.0 47.4 %collective-permute-start.53 = (bf16[512,1024]{1,0:T(8,128)(2,1)S(1)}, bf16[512,1024]{1,0:T(8,128)(2,1)}, u32[]{:S(2)}, u32[]{:S(2)}) collective-permute-start(bf16[512,1024]{1,0:T(8,128)(2,1)S(1)} %add_convert_fusion.26), channel_id=1, source_target_pairs={{8,16},{16,8},{9,17},{17,9},{10,18},{18,10},{11,19},{19,11},{12,20... | collective-permute-start | bytes 3145736 | tf_op jit(solution)/shard_map/ppermute | solution.py:153
  543.2 44.8 %collective-permute-start.52 = (bf16[512,1024]{1,0:T(8,128)(2,1)}, bf16[512,1024]{1,0:T(8,128)(2,1)S(1)}, u32[]{:S(2)}, u32[]{:S(2)}) collective-permute-start(bf16[512,1024]{1,0:T(8,128)(2,1)} %get-tuple-element.1292), channel_id=1, source_target_pairs={{0,8},{8,0},{16,24},{24,16},{1,9},{9,1},{17,25},{25,17},{2,10},{10... | collective-permute-start | bytes 3145736 | tf_op jit(solution)/shard_map/ppermute | solution.py:141
  560.4 51.2 %collective-permute-start.58 = (bf16[512,1024]{1,0:T(8,128)(2,1)}, bf16[512,1024]{1,0:T(8,128)(2,1)}, u32[]{:S(2)}, u32[]{:S(2)}) collective-permute-start(bf16[512,1024]{1,0:T(8,128)(2,1)} %convolution_convert_fusion.11), channel_id=1, source_target_pairs={{0,1},{1,0},{2,3},{3,2},{4,5},{5,4},{6,7},{7,6},{8,9},{9,8},{10,11... | collective-permute-start | bytes 3145736 | tf_op jit(solution)/shard_map/ppermute | solution.py:47
  594.7 45.2 %collective-permute-start.55 = (bf16[512,1024]{1,0:T(8,128)(2,1)}, bf16[512,1024]{1,0:T(8,128)(2,1)}, u32[]{:S(2)}, u32[]{:S(2)}) collective-permute-start(bf16[512,1024]{1,0:T(8,128)(2,1)} %convolution_convert_fusion.9), channel_id=1, source_target_pairs={{0,1},{1,0},{2,3},{3,2},{4,5},{5,4},{6,7},{7,6},{8,9},{9,8},{10,11... | collective-permute-start | bytes 3145736 | tf_op jit(solution)/shard_map/ppermute | solution.py:47
  624.8 39.2 %collective-permute-start.64 = (bf16[512,1024]{1,0:T(8,128)(2,1)}, bf16[512,1024]{1,0:T(8,128)(2,1)}, u32[]{:S(2)}, u32[]{:S(2)}) collective-permute-start(bf16[512,1024]{1,0:T(8,128)(2,1)} %convolution_convert_fusion.7), channel_id=1, source_target_pairs={{0,1},{1,0},{2,3},{3,2},{4,5},{5,4},{6,7},{7,6},{8,9},{9,8},{10,11... | collective-permute-start | bytes 3145736 | tf_op jit(solution)/shard_map/ppermute | solution.py:47
  644.7 37.5 %collective-permute-start.74 = (bf16[256,1024]{1,0:T(8,128)(2,1)S(1)}, bf16[256,1024]{1,0:T(8,128)(2,1)S(1)}, u32[]{:S(2)}, u32[]{:S(2)}) collective-permute-start(bf16[256,1024]{1,0:T(8,128)(2,1)S(1)} %get-tuple-element.1639), channel_id=1, source_target_pairs={{1,4},{3,6},{4,1},{6,3},{9,12},{11,14},{12,9},{14,11},{17,20},{19,... | collective-permute-start | bytes 1572872 | tf_op jit(solution)/shard_map/ppermute | solution.py:47
  684.0 40.2 %collective-permute-start.81 = (bf16[512,1024]{1,0:T(8,128)(2,1)S(1)}, bf16[512,1024]{1,0:T(8,128)(2,1)S(1)}, u32[]{:S(2)}, u32[]{:S(2)}) collective-permute-start(bf16[512,1024]{1,0:T(8,128)(2,1)S(1)} %convolution_convert_fusion.3), channel_id=1, source_target_pairs={{0,1},{1,0},{2,3},{3,2},{4,5},{5,4},{6,7},{7,6},{8,9},{9,8},{10,11... | collective-permute-start | bytes 3145736 | tf_op jit(solution)/shard_map/ppermute | solution.py:47
  743.8 48.9 %collective-permute-start.86 = (bf16[512,1024]{1,0:T(8,128)(2,1)S(1)}, bf16[512,1024]{1,0:T(8,128)(2,1)S(1)}, u32[]{:S(2)}, u32[]{:S(2)}) collective-permute-start(bf16[512,1024]{1,0:T(8,128)(2,1)S(1)} %add_convert_fusion.4), channel_id=1, source_target_pairs={{0,8},{8,0},{16,24},{24,16},{1,9},{9,1},{17,25},{25,17},{2,10},{10... | collective-permute-start | bytes 3145736 | tf_op jit(solution)/shard_map/ppermute | solution.py:143
  767.3 42.6 %collective-permute-start.85 = (bf16[512,1024]{1,0:T(8,128)(2,1)S(1)}, bf16[512,1024]{1,0:T(8,128)(2,1)S(1)}, u32[]{:S(2)}, u32[]{:S(2)}) collective-permute-start(bf16[512,1024]{1,0:T(8,128)(2,1)S(1)} %add_convert_fusion.2), channel_id=1, source_target_pairs={{0,8},{8,0},{16,24},{24,16},{1,9},{9,1},{17,25},{25,17},{2,10},{10... | collective-permute-start | bytes 3145736 | tf_op jit(solution)/shard_map/ppermute | solution.py:143
  772.8 57.7 %collective-permute-start.88 = (bf16[512,1024]{1,0:T(8,128)(2,1)S(1)}, bf16[512,1024]{1,0:T(8,128)(2,1)S(1)}, u32[]{:S(2)}, u32[]{:S(2)}) collective-permute-start(bf16[512,1024]{1,0:T(8,128)(2,1)S(1)} %add_convert_fusion.1), channel_id=1, source_target_pairs={{0,8},{8,0},{16,24},{24,16},{1,9},{9,1},{17,25},{25,17},{2,10},{10... | collective-permute-start | bytes 3145736 | tf_op jit(solution)/shard_map/ppermute | solution.py:143
  (187 other events, 2763.9 us)

commit v3 on v2

--- a/solution.py
+++ b/solution.py
@@ -1,6 +1,8 @@
 import jax
 import jax.numpy as jnp
 from jax import lax
+from jax.experimental import pallas as pl
+from jax.experimental.pallas import tpu as pltpu
 from jax.sharding import PartitionSpec as P
 
 LEN = 1024
@@ -87,6 +89,145 @@
     half = values.shape[1] // 2
     front, back = values[:, :half], values[:, half:]
     return jnp.concatenate((front * cosine + back * sine, back * cosine - front * sine), 1)
+
+
+VMEM_BYTES = 56 * 1024 * 1024
+BLOCK = 256
+
+
+def call(body, grid, ins, in_specs, outs, out_specs, scratch=()):
+    return pl.pallas_call(
+        body,
+        grid=grid,
+        in_specs=in_specs,
+        out_specs=out_specs,
+        out_shape=outs,
+        scratch_shapes=list(scratch),
+        compiler_params=pltpu.CompilerParams(
+            vmem_limit_bytes=VMEM_BYTES, dimension_semantics=("arbitrary",) * len(grid)
+        ),
+    )(*ins)
+
+
+SCALARS = pl.BlockSpec(memory_space=pltpu.SMEM)
+
+
+def decay_block(scalars, rates, head, i, j):
+    base = scalars[0]
+    apart = ((base ^ i) - (base ^ j)) * BLOCK
+    distance = (
+        apart
+        + lax.broadcasted_iota(jnp.int32, (BLOCK, BLOCK), 0)
+        - lax.broadcasted_iota(jnp.int32, (BLOCK, BLOCK), 1)
+    )
+    lag = jnp.maximum(distance, 0).astype(F32)
+    return jnp.where(distance >= 0, jnp.exp(-rates[head] * lag), 0.0)
+
+
+def retention(scalars, rates, query, key, value):
+    tokens = query.shape[0]
+    size, out_size = query.shape[1] // 2, value.shape[1] // 2
+    blocks = tokens // BLOCK
+
+    def body(scalar_ref, rate_ref, q_ref, k_ref, v_ref, normed_ref, inverse_ref, open_ref, sums):
+        head = pl.program_id(0)
+        base = scalar_ref[0]
+        for i in range(blocks):
+            rows = pl.ds(i * BLOCK, BLOCK)
+            sums[...] = jnp.zeros(sums.shape, F32)
+            q = q_ref[rows, :]
+            for j in range(blocks):
+                @pl.when((base ^ i) >= (base ^ j))
+                def _():
+                    columns = pl.ds(j * BLOCK, BLOCK)
+                    mask = decay_block(scalar_ref, rate_ref, head, i, j)
+                    weighted = (contract_cols(q, k_ref[columns, :]) * mask).astype(BF)
+                    sums[...] += dot(weighted, v_ref[columns, :])
+
+            total = sums[...]
+            average = jnp.mean(total, 1, keepdims=True)
+            centred = total - average
+            variance = jnp.mean(centred * centred, 1, keepdims=True)
+            inverse = lax.rsqrt(jnp.maximum(variance, 1.0))
+            normed_ref[rows, :] = centred * inverse
+            inverse_ref[0, rows, :] = inverse
+            open_ref[0, rows, :] = jnp.where(variance > 1.0, 1.0, 0.0)
+
+    head_block = lambda columns: pl.BlockSpec((tokens, columns), lambda h: (0, h))
+    column = pl.BlockSpec((1, tokens, 1), lambda h: (h, 0, 0))
+    return call(
+        body,
+        (2,),
+        [scalars, rates, query, key, value],
+        [SCALARS, SCALARS, head_block(size), head_block(size), head_block(out_size)],
+        [
+            jax.ShapeDtypeStruct((tokens, 2 * out_size), F32),
+            jax.ShapeDtypeStruct((2, tokens, 1), F32),
+            jax.ShapeDtypeStruct((2, tokens, 1), F32),
+        ],
+        [head_block(out_size), column, column],
+        [pltpu.VMEM((BLOCK, out_size), F32)],
+    )
+
+
+def retention_back(scalars, rates, query, key, value, grad, cosine, sine):
+    tokens = query.shape[0]
+    size, out_size = query.shape[1] // 2, value.shape[1] // 2
+    blocks = tokens // BLOCK
+
+    def body(
+        scalar_ref, rate_ref, q_ref, k_ref, v_ref, g_ref, cos_ref, sin_ref,
+        gv_ref, gq_ref, gk_ref, q_sum, k_sum, v_sum,
+    ):
+        head = pl.program_id(0)
+        base = scalar_ref[0]
+        k_sum[...] = jnp.zeros(k_sum.shape, F32)
+        v_sum[...] = jnp.zeros(v_sum.shape, F32)
+        for i in range(blocks):
+            rows = pl.ds(i * BLOCK, BLOCK)
+            q_sum[...] = jnp.zeros(q_sum.shape, F32)
+            q, g = q_ref[rows, :], g_ref[rows, :]
+            for j in range(blocks):
+                @pl.when((base ^ i) >= (base ^ j))
+                def _():
+                    columns = pl.ds(j * BLOCK, BLOCK)
+                    mask = decay_block(scalar_ref, rate_ref, head, i, j)
+                    k = k_ref[columns, :]
+                    weighted = (contract_cols(q, k) * mask).astype(BF)
+                    v_sum[columns, :] += contract_rows(weighted, g)
+                    scores = (contract_cols(g, v_ref[columns, :]) * mask).astype(BF)
+                    q_sum[...] += dot(scores, k)
+                    k_sum[columns, :] += contract_rows(scores, q)
+
+            gq_ref[rows, :] = rotate_back(q_sum[...], cos_ref[rows, :], sin_ref[rows, :]).astype(BF)
+        for j in range(blocks):
+            columns = pl.ds(j * BLOCK, BLOCK)
+            gk_ref[columns, :] = rotate_back(
+                k_sum[columns, :], cos_ref[columns, :], sin_ref[columns, :]
+            ).astype(BF)
+            gv_ref[columns, :] = v_sum[columns, :].astype(BF)
+
+    head_block = lambda columns: pl.BlockSpec((tokens, columns), lambda h: (0, h))
+    table = pl.BlockSpec(cosine.shape, lambda h: (0, 0))
+    return call(
+        body,
+        (2,),
+        [scalars, rates, query, key, value, grad, cosine, sine],
+        [SCALARS, SCALARS, head_block(size), head_block(size)]
+        + [head_block(out_size)] * 2
+        + [table, table],
+        [
+            jax.ShapeDtypeStruct((tokens, 2 * out_size), BF),
+            jax.ShapeDtypeStruct((tokens, 2 * size), BF),
+            jax.ShapeDtypeStruct((tokens, 2 * size), BF),
+        ],
+        [head_block(out_size), head_block(size), head_block(size)],
+        [
+            pltpu.VMEM((BLOCK, size), F32),
+            pltpu.VMEM((tokens, size), F32),
+            pltpu.VMEM((tokens, out_size), F32),
+        ],
+    )
 
 
 OUTER = [(0, 1), (1, 0), (2, 3), (3, 2)]
@@ -222,6 +363,7 @@
     small = jnp.concatenate((first_gain, second_gain, group_gain, decay_rate))
     small_other = move(small, TO_COL)
     line = Line()
+    scalars = jnp.stack([2 * k + x, parity, x, k]).astype(jnp.int32)
     step, take = line.step, line.take
 
     count = lax.axis_size("dp")
@@ -279,7 +421,7 @@
     own_group = (group_gain, small_other[2 * width : 2 * width + head_values])
     own_rate = (decay_rate[0], small_other[2 * width + head_values])
     group_gains = tuple(jnp.where(y == 0, own_group[i], own_group[1 - i]) for i in range(2))
-    rates = tuple(jnp.where(y == 0, own_rate[i], own_rate[1 - i]) for i in range(2))
+    rates = jnp.stack([jnp.where(y == 0, own_rate[i], own_rate[1 - i]) for i in range(2)])
 
     query_key_half = take(query_key_half)
     query_key_swap = over_dp(query_key_half)
@@ -301,41 +443,29 @@
     value_swap = over_dp(value_half)
     output_half = over_col(output_send)
 
-    masks = step(
-        lambda far, near: tuple(
-            jnp.where(near >= 0, jnp.exp(-rate * far), 0.0) for rate in rates
-        ),
-        lag,
-        distance,
-    )
-
     def other_query_key(rows, half, swapped, query, key, cos, sin):
         other = join_halves(half, swapped)
         rows = rows[:, width:]
         query = query + dot(rows, other[:, :head_cols])
         key = key + dot(rows, other[:, head_cols:])
         out = [other]
-        for head in range(2):
-            cut = slice(head * key_size, (head + 1) * key_size)
-            out.append(rotate(query[:, cut], cos, sin).astype(BF))
-            out.append(rotate(key[:, cut], cos, sin).astype(BF))
+        for total in (query, key):
+            out.append(
+                jnp.concatenate(
+                    [
+                        rotate(total[:, h * key_size : (h + 1) * key_size], cos, sin)
+                        for h in range(2)
+                    ],
+                    1,
+                ).astype(BF)
+            )
         return tuple(out)
 
-    query_key_other, *turned = step(
+    query_key_other, query_rot, key_rot = step(
         other_query_key, first_in, query_key_half, query_key_swap, query_mine, key_mine, cosine, sine
     )
-    query_rot, key_rot = turned[::2], turned[1::2]
     query_other, key_other = query_key_other[:, :head_cols], query_key_other[:, head_cols:]
 
-    scores = [
-        step(
-            lambda q, w, m: (contract_cols(q, w) * m).astype(BF),
-            query_rot[head],
-            key_rot[head],
-            masks[head],
-        )
-        for head in range(2)
-    ]
     swish_half = take(swish_half)
     swish_swap = over_dp(swish_half)
 
@@ -347,42 +477,22 @@
     grad_held = take(grad_out)
     grad_seq, grad_cross = move(grad_held, SEQ_IN), move(grad_held, CROSS)
 
-    def retain(weighted, value):
-        retained = dot(weighted, value)
-        average = jnp.mean(retained, 1, keepdims=True)
-        centred = retained - average
-        variance = jnp.mean(centred * centred, 1, keepdims=True)
-        inverse = lax.rsqrt(jnp.maximum(variance, 1.0))
-        return centred * inverse, inverse, (variance > 1.0).astype(F32)
-
-    retained = [step(retain, scores[0], valued[:, values[0]])]
+    normed, group_inv, group_open = step(
+        lambda *held: tuple(retention(scalars, rates, *held)), query_rot, key_rot, valued
+    )
     output_half = take(output_half)
     output_swap = over_dp(output_half)
     gate_half = over_col(step(send_half, gate_weight))
-    retained.append(step(retain, scores[1], valued[:, values[1]]))
-
-    def gating(rows, half, swapped, swish, first_normed, second_normed, gain0, gain1):
+
+    wide_gain = jnp.concatenate(group_gains)
+
+    def gating(rows, half, swapped, mine, normed, gains):
         other = join_halves(half, swapped)
-        swish = swish + dot(rows[:, width:], other)
-        gate = jax.nn.silu(swish)
-        gated = jnp.concatenate(
-            (
-                gate[:, values[0]] * first_normed * gain0,
-                gate[:, values[1]] * second_normed * gain1,
-            ),
-            1,
-        )
-        return other, swish, gated.astype(BF)
+        swish = mine + dot(rows[:, width:], other)
+        return other, swish, (jax.nn.silu(swish) * normed * gains).astype(BF)
 
     swish_other, swish_in, gated = step(
-        gating,
-        first_in,
-        swish_half,
-        swish_swap,
-        swish_mine,
-        retained[0][0],
-        retained[1][0],
-        *group_gains,
+        gating, first_in, swish_half, swish_swap, swish_mine, normed, wide_gain
     )
     up_half = over_col(step(send_half, up_weight))
     grad_half = step(sequence_rows, grad_out, grad_seq, grad_cross)
@@ -478,7 +588,6 @@
         return tile
 
     totals.start(tile_out(0), hidden, grad_rows)
-    totals.start(tile_out(1), hidden, grad_rows)
     down_other = step(join_halves, down_half, down_swap)
 
     def feed_back(grads, gate, up, down_o):
@@ -489,6 +598,7 @@
         return pull(grad_hidden * up)[0].astype(BF), (grad_hidden * value).astype(BF)
 
     grad_gate, grad_up = step(feed_back, grad_rows, gate_pre, up_pre, down_other)
+    totals.start(tile_out(1), hidden, grad_rows)
 
     def back_half(rows, low, terms):
         flat = [value for term in terms for value in term]
@@ -564,7 +674,9 @@
             grad_gated[:, values[head]],
             swish_in[:, values[head]],
             group_gains[head],
-            *retained[head],
+            normed[:, values[head]],
+            group_inv[head],
+            group_open[head],
         )
         for head in range(2)
     ]
@@ -573,42 +685,16 @@
     totals.turn(5)
     totals.start(tile_out(1), gated, attn_in)
 
-    def retain_back(grad, weighted, value, mask, q, w, cos, sin):
-        grad_value = contract_rows(weighted, grad).astype(BF)
-        grad_scores = (contract_cols(grad, value) * mask).astype(BF)
-        return (
-            grad_value,
-            rotate_back(dot(grad_scores, w), cos, sin).astype(BF),
-            rotate_back(contract_rows(grad_scores, q), cos, sin).astype(BF),
-        )
-
-    backs = []
-    for head in range(2):
-        backs.append(
-            step(
-                retain_back,
-                heads[head][2],
-                scores[head],
-                valued[:, values[head]],
-                masks[head],
-                query_rot[head],
-                key_rot[head],
-                cosine,
-                sine,
-            )
-        )
-        totals.turn(6 + head)
-        totals.start(tile_in(head), first_in, grad_swish)
-    grad_value, grad_query, grad_key, grad_query_key = step(
-        lambda v0, q0, k0, v1, q1, k1: (
-            jnp.concatenate((v0, v1), 1),
-            jnp.concatenate((q0, q1), 1),
-            jnp.concatenate((k0, k1), 1),
-            jnp.concatenate((q0, q1, k0, k1), 1),
-        ),
-        *backs[0],
-        *backs[1],
-    )
+    grad_retained = step(lambda a, b: jnp.concatenate((a, b), 1), heads[0][2], heads[1][2])
+    totals.turn(6)
+    totals.start(tile_in(0), first_in, grad_swish)
+    grad_value, grad_query, grad_key = step(
+        lambda *held: tuple(retention_back(scalars, rates, *held)),
+        query_rot, key_rot, valued, grad_retained, cosine, sine,
+    )
+    totals.turn(7)
+    totals.start(tile_in(1), first_in, grad_swish)
+    grad_query_key = step(lambda a, b: jnp.concatenate((a, b), 1), grad_query, grad_key)
     head_terms = (
         (grad_query, query_weight, query_other),
         (grad_key, key_weight, key_other),

time: 845 us -> 841 us (level)
  Pallas kernels: 0 us -> 32.4 us
  starting transfers between devices: 172 us -> 158 us
  local copies, waits for them, and re-layouts: 67.1 us -> 57.8 us
    pallas_call x0 -> x2, Pallas kernels: none -> 32.4 us  [call(): pl.pallas_call(body, grid=grid, in_specs=in_specs, out_specs=out_specs, o...]
    ppermute x14, waiting for transfers between devices: 91.8 us -> 71.1 us  [turn(): self.got.append(lax.ppermute(sent, 'dp', OUTER))]
    ppermute x14, starting transfers between devices: 57.5 us -> 43.7 us  [turn(): self.got.append(lax.ppermute(sent, 'dp', OUTER))]
    ppermute x49, waiting for transfers between devices: 150 us -> 162 us  [move(): return lax.ppermute(value, RC, pairs)]
    dot_general x24 -> x20, matrix products: 52.3 us -> 45.4 us  [dot(): return jnp.dot(left, right, preferred_element_type=F32)]
    unnamed x247 -> x195, local copies, waits for them, and re-layouts: 36.6 us -> 29.8 us
    dot_general x32 -> x28, matrix products: 49.7 us -> 53 us  [contract_rows(): lax.dot_general(left, right, (((0,), (0,)), ((), ())), preferred_element_...]
    dot_general x32 -> x28, matrix products: 51.9 us -> 51.7 us  [contract_cols(): lax.dot_general(left, right, (((1,), (1,)), ((), ())), preferred_element_...]
  transfers between devices with their start and end apart: 89 -> 89, of which waited for: 32 -> 34; matrix products, arithmetic and copies ran while one was open for 38% -> 35% of each run, Pallas kernels for 0% -> 4%
where the time goes in v3:
time: 841 us; the launch traced here: 829 us
  waiting for transfers between devices  281 us (33%)
  starting transfers between devices  158 us (19%)
  matrix products  150 us (18%)
  other arithmetic  145 us (17%)
  local copies, waits for them, and re-layouts  57.8 us (7%)
  Pallas kernels  32.4 us (4%)
    ppermute x49, waiting for transfers between devices, move(): return lax.ppermute(value, RC, pairs)  162 us
    ppermute x14, waiting for transfers between devices, turn(): self.got.append(lax.ppermute(sent, 'dp', OUTER))  71.1 us
    ppermute x49, starting transfers between devices, move(): return lax.ppermute(value, RC, pairs)  59.3 us
    dot_general x28, matrix products, contract_rows(): lax.dot_general(left, right, (((0,), (0,)), ((), ())), preferred_element_...  53 us
    dot_general x28, matrix products, contract_cols(): lax.dot_general(left, right, (((1,), (1,)), ((), ())), preferred_element_...  51.7 us
    dot_general x20, matrix products, dot(): return jnp.dot(left, right, preferred_element_type=F32)  45.4 us
    ppermute x14, starting transfers between devices, turn(): self.got.append(lax.ppermute(sent, 'dp', OUTER))  43.7 us
    ppermute x3, waiting for transfers between devices, turn(): self.got.append(lax.ppermute(self.totals[back], 'dp', OUTER))  34.9 us
  transfers between devices with their start and end apart: 89, of which 34 were waited for; matrix products, arithmetic and copies ran while one was open for 35% of the time, Pallas kernels for 4%

profile of v3, /device:TPU:0, one launch (start us, length us, event | category | flops | bytes accessed | tf_op | source)
XLA Modules:
  0.0 829.4 jit_solution(16352011007839313561)
XLA Ops:
  15.8 11.6 %collective-permute-done.2 = f32[2561]{0:T(1024)S(1)} collective-permute-done((f32[2561]{0:T(1024)S(1)}, f32[2561]{0:T(1024)S(1)}, u32[]{:S(2)}, u32[]{:S(2)}) %collective-permute-start.2) | collective-permute-done | bytes 10276 | tf_op jit(solution)/shard_map/ppermute | solution.py:49
  44.7 19.4 %collective-permute-done.4 = bf16[512,1024]{1,0:T(8,128)(2,1)} collective-permute-done((bf16[512,1024]{1,0:T(8,128)(2,1)}, bf16[512,1024]{1,0:T(8,128)(2,1)}, u32[]{:S(2)}, u32[]{:S(2)}) %collective-permute-start.4) | collective-permute-done | bytes 1048608 | tf_op jit(solution)/shard_map/ppermute | solution.py:49
  101.5 7.5 collective-permute-done.5
  126.5 14.1 %shard_map.237 = (f32[1024,1024]{1,0:T(8,128)}, f32[2,1024,1]{2,1,0:T(8,128)}, f32[2,1024,1]{2,1,0:T(8,128)}) custom-call(s32[4]{0:T(128)} %pad_add_fusion.scalar_ref, f32[2]{0:T(128)} %pad_maximum_fusion.36.rate_ref, bf16[1024,512]{1,0:T(8,128)(2,1)} %get-tuple-element.1171.q_ref, bf16[1024,512]{1,0:T(8,128)(2,1)} %get-tuple-element.1172.k_ref, ...), custom_call_target="tpu_custom_call" | custom-call | tf_op jit(solution)/shard_map/pallas_call | solution.py:99
  140.6 12.4 %collective-permute-done.10 = bf16[512,1024]{1,0:T(8,128)(2,1)} collective-permute-done((bf16[512,1024]{1,0:T(8,128)(2,1)}, bf16[512,1024]{1,0:T(8,128)(2,1)}, u32[]{:S(2)}, u32[]{:S(2)}) %collective-permute-start.10) | collective-permute-done | bytes 1048608 | tf_op jit(solution)/shard_map/ppermute | solution.py:49
  206.4 18.1 %collective-permute-done.16 = bf16[256,2048]{1,0:T(8,128)(2,1)} collective-permute-done((bf16[256,2048]{1,0:T(8,128)(2,1)}, bf16[256,2048]{1,0:T(8,128)(2,1)}, u32[]{:S(2)}, u32[]{:S(2)}) %collective-permute-start.16) | collective-permute-done | bytes 1048608 | tf_op jit(solution)/shard_map/ppermute | solution.py:49
  234.7 17.1 %collective-permute-done.18 = bf16[256,2048]{1,0:T(8,128)(2,1)S(1)} collective-permute-done((bf16[256,2048]{1,0:T(8,128)(2,1)S(1)}, bf16[256,2048]{1,0:T(8,128)(2,1)S(1)}, u32[]{:S(2)}, u32[]{:S(2)}) %collective-permute-start.18) | collective-permute-done | bytes 1048608 | tf_op jit(solution)/shard_map/ppermute | solution.py:49
  271.1 7.8 fusion.15
  289.4 8.4 %multiply_convert_fusion = (bf16[1024,1024]{1,0:T(8,128)(2,1)S(1)}, bf16[1024,1024]{1,0:T(8,128)(2,1)S(1)}) fusion(f32[1024,1024]{1,0:T(8,128)} %copy-done.92, f32[1024,1024]{1,0:T(8,128)} %get-tuple-element.933, f32[1024,1024]{1,0:T(8,128)} %fusion.40, bf16[1024,1024]{1,0:T(8,128)(2,1)S(1)} %copy-done, bf16[1024,2048]{1,0:T(8,128)(2,1)S(1)} %pad_maximum_fusion.1), kind=kOutput, calls=%fused_computation.33 | convolution fusion | flops 2173698048 | bytes 20971520 | tf_op jit(solution)/shard_map/dot_general | solution.py:61
  312.8 17.1 %collective-permute-done.26 = bf16[512,1024]{1,0:T(8,128)(2,1)S(1)} collective-permute-done((bf16[512,1024]{1,0:T(8,128)(2,1)S(1)}, bf16[512,1024]{1,0:T(8,128)(2,1)S(1)}, u32[]{:S(2)}, u32[]{:S(2)}) %collective-permute-start.26) | collective-permute-done | bytes 1048608 | tf_op jit(solution)/shard_map/ppermute | solution.py:49
  366.9 7.4 collective-permute-done.28
  377.7 7.6 collective-permute-done.33
  393.8 11.4 %collective-permute-done.31 = bf16[256,2048]{1,0:T(8,128)(2,1)S(1)} collective-permute-done((bf16[256,2048]{1,0:T(8,128)(2,1)S(1)}, bf16[256,2048]{1,0:T(8,128)(2,1)S(1)}, u32[]{:S(2)}, u32[]{:S(2)}) %collective-permute-start.31) | collective-permute-done | bytes 1048608 | tf_op jit(solution)/shard_map/ppermute | solution.py:49
  432.1 10.8 %collective-permute-done.40 = bf16[512,1024]{1,0:T(8,128)(2,1)S(1)} collective-permute-done((bf16[512,1024]{1,0:T(8,128)(2,1)}, bf16[512,1024]{1,0:T(8,128)(2,1)S(1)}, u32[]{:S(2)}, u32[]{:S(2)}) %collective-permute-start.40) | collective-permute-done | bytes 1048608 | tf_op jit(solution)/shard_map/ppermute | solution.py:282
  463.4 16.4 %collective-permute-done.43 = bf16[512,1024]{1,0:T(8,128)(2,1)S(1)} collective-permute-done((bf16[512,1024]{1,0:T(8,128)(2,1)S(1)}, bf16[512,1024]{1,0:T(8,128)(2,1)S(1)}, u32[]{:S(2)}, u32[]{:S(2)}) %collective-permute-start.43) | collective-permute-done | bytes 1048608 | tf_op jit(solution)/shard_map/ppermute | solution.py:282
  515.9 18.3 %shard_map.238 = (bf16[1024,1024]{1,0:T(8,128)(2,1)}, bf16[1024,512]{1,0:T(8,128)(2,1)}, bf16[1024,512]{1,0:T(8,128)(2,1)}) custom-call(s32[4]{0:T(128)} %pad_add_fusion.scalar_ref, f32[2]{0:T(128)} %pad_maximum_fusion.36.rate_ref, bf16[1024,512]{1,0:T(8,128)(2,1)} %get-tuple-element.1171.q_ref, bf16[1024,512]{1,0:T(8,128)(2,1)} %get-tuple-element.1172.k_ref, ...), custom_call_target="tpu_custom_call" | custom-call | tf_op jit(solution)/shard_map/pallas_call | solution.py:99
  689.3 8.4 %collective-permute-done.70 = bf16[512,1024]{1,0:T(8,128)(2,1)S(1)} collective-permute-done((bf16[512,1024]{1,0:T(8,128)(2,1)S(1)}, bf16[512,1024]{1,0:T(8,128)(2,1)S(1)}, u32[]{:S(2)}, u32[]{:S(2)}) %collective-permute-start.70) | collective-permute-done | bytes 1048608 | tf_op jit(solution)/shard_map/ppermute | solution.py:49
  701.9 8.1 collective-permute-start.80
  711.0 8.9 %collective-permute-done.67 = bf16[256,2048]{1,0:T(8,128)(2,1)S(1)} collective-permute-done((bf16[256,2048]{1,0:T(8,128)(2,1)S(1)}, bf16[256,2048]{1,0:T(8,128)(2,1)S(1)}, u32[]{:S(2)}, u32[]{:S(2)}) %collective-permute-start.67) | collective-permute-done | bytes 1048608 | tf_op jit(solution)/shard_map/ppermute | solution.py:49
  721.3 11.6 %collective-permute-done.80 = bf16[512,1024]{1,0:T(8,128)(2,1)S(1)} collective-permute-done((bf16[512,1024]{1,0:T(8,128)(2,1)S(1)}, bf16[512,1024]{1,0:T(8,128)(2,1)S(1)}, u32[]{:S(2)}, u32[]{:S(2)}) %collective-permute-start.80) | collective-permute-done | bytes 1048608 | tf_op jit(solution)/shard_map/ppermute | solution.py:282
  745.0 16.1 %collective-permute-done.83 = bf16[512,1024]{1,0:T(8,128)(2,1)S(1)} collective-permute-done((bf16[512,1024]{1,0:T(8,128)(2,1)S(1)}, bf16[512,1024]{1,0:T(8,128)(2,1)S(1)}, u32[]{:S(2)}, u32[]{:S(2)}) %collective-permute-start.83) | collective-permute-done | bytes 1048608 | tf_op jit(solution)/shard_map/ppermute | solution.py:282
  768.7 18.4 %collective-permute-start.88 = (bf16[512,1024]{1,0:T(8,128)(2,1)S(1)}, bf16[512,1024]{1,0:T(8,128)(2,1)S(1)}, u32[]{:S(2)}, u32[]{:S(2)}) collective-permute-start(bf16[512,1024]{1,0:T(8,128)(2,1)S(1)} %add_convert_fusion.1), channel_id=1, source_target_pairs={{0,8},{8,0},{16,24},{24,16},{1,9},{9,1},{17,25},{25,17},{2,10},{10... | collective-permute-start | bytes 3145736 | tf_op jit(solution)/shard_map/ppermute | solution.py:284
  788.7 17.3 %collective-permute-done.85 = bf16[512,1024]{1,0:T(8,128)(2,1)S(1)} collective-permute-done((bf16[512,1024]{1,0:T(8,128)(2,1)S(1)}, bf16[512,1024]{1,0:T(8,128)(2,1)S(1)}, u32[]{:S(2)}, u32[]{:S(2)}) %collective-permute-start.85) | collective-permute-done | bytes 1048608 | tf_op jit(solution)/shard_map/ppermute | solution.py:284
  808.9 17.6 %collective-permute-done.88 = bf16[512,1024]{1,0:T(8,128)(2,1)S(1)} collective-permute-done((bf16[512,1024]{1,0:T(8,128)(2,1)S(1)}, bf16[512,1024]{1,0:T(8,128)(2,1)S(1)}, u32[]{:S(2)}, u32[]{:S(2)}) %collective-permute-start.88) | collective-permute-done | bytes 1048608 | tf_op jit(solution)/shard_map/ppermute | solution.py:284
  (632 shorter events, 512.7 us)
Async XLA Ops:
  39.7 46.8 %collective-permute-start.7 = (bf16[512,1024]{1,0:T(8,128)(2,1)}, bf16[512,1024]{1,0:T(8,128)(2,1)}, u32[]{:S(2)}, u32[]{:S(2)}) collective-permute-start(bf16[512,1024]{1,0:T(8,128)(2,1)} %constant_dynamic-slice_fusion.5), channel_id=1, source_target_pairs={{0,1},{1,0},{2,3},{3,2},{4,5},{5,4},{6,7},{7,6},{8,9},{9,8},{10,11... | collective-permute-start | bytes 3145736 | tf_op jit(solution)/shard_map/ppermute | solution.py:49
  65.8 43.2 %collective-permute-start.5 = (bf16[512,1024]{1,0:T(8,128)(2,1)S(1)}, bf16[512,1024]{1,0:T(8,128)(2,1)}, u32[]{:S(2)}, u32[]{:S(2)}) collective-permute-start(bf16[512,1024]{1,0:T(8,128)(2,1)S(1)} %constant_dynamic-slice_fusion.4), channel_id=1, source_target_pairs={{0,1},{1,0},{2,3},{3,2},{4,5},{5,4},{6,7},{7,6},{8,9},{9,8},{10,11... | collective-permute-start | bytes 3145736 | tf_op jit(solution)/shard_map/ppermute | solution.py:49
  90.8 62.2 %collective-permute-start.10 = (bf16[512,1024]{1,0:T(8,128)(2,1)}, bf16[512,1024]{1,0:T(8,128)(2,1)}, u32[]{:S(2)}, u32[]{:S(2)}) collective-permute-start(bf16[512,1024]{1,0:T(8,128)(2,1)} %constant_dynamic-slice_fusion.3), channel_id=1, source_target_pairs={{0,1},{1,0},{2,3},{3,2},{4,5},{5,4},{6,7},{7,6},{8,9},{9,8},{10,11... | collective-permute-start | bytes 3145736 | tf_op jit(solution)/shard_map/ppermute | solution.py:49
  109.0 46.3 %collective-permute-start.8 = (bf16[512,1024]{1,0:T(8,128)(2,1)}, bf16[512,1024]{1,0:T(8,128)(2,1)}, u32[]{:S(2)}, u32[]{:S(2)}) collective-permute-start(bf16[512,1024]{1,0:T(8,128)(2,1)} %collective-permute-done.5), channel_id=1, source_target_pairs={{0,8},{8,0},{16,24},{24,16},{1,9},{9,1},{17,25},{25,17},{2,10},{10... | collective-permute-start | bytes 3145736 | tf_op jit(solution)/shard_map/ppermute | solution.py:383
  122.4 54.0 %collective-permute-start.13 = (bf16[512,1024]{1,0:T(8,128)(2,1)}, bf16[512,1024]{1,0:T(8,128)(2,1)}, u32[]{:S(2)}, u32[]{:S(2)}) collective-permute-start(bf16[512,1024]{1,0:T(8,128)(2,1)} %param.15), channel_id=1, source_target_pairs={{1,4},{3,6},{4,1},{6,3},{9,12},{11,14},{12,9},{14,11},{17,20},{19,... | collective-permute-start | bytes 3145736 | tf_op jit(solution)/shard_map/ppermute | solution.py:49
  124.1 52.4 %collective-permute-start.12 = (bf16[512,1024]{1,0:T(8,128)(2,1)}, bf16[512,1024]{1,0:T(8,128)(2,1)}, u32[]{:S(2)}, u32[]{:S(2)}) collective-permute-start(bf16[512,1024]{1,0:T(8,128)(2,1)} %param.15), channel_id=1, source_target_pairs={{0,4},{1,0},{2,6},{3,2},{4,5},{5,1},{6,7},{7,3},{8,12},{9,8},{10,1... | collective-permute-start | bytes 3145736 | tf_op jit(solution)/shard_map/ppermute | solution.py:49
  304.1 48.4 %collective-permute-start.30 = (bf16[512,1024]{1,0:T(8,128)(2,1)}, bf16[512,1024]{1,0:T(8,128)(2,1)}, u32[]{:S(2)}, u32[]{:S(2)}) collective-permute-start(bf16[512,1024]{1,0:T(8,128)(2,1)} %fusion.74), channel_id=1, source_target_pairs={{0,1},{1,0},{2,3},{3,2},{4,5},{5,4},{6,7},{7,6},{8,9},{9,8},{10,11... | collective-permute-start | bytes 3145736 | tf_op jit(solution)/shard_map/ppermute | solution.py:49
  333.8 43.4 %collective-permute-start.34 = (bf16[512,1024]{1,0:T(8,128)(2,1)}, bf16[512,1024]{1,0:T(8,128)(2,1)S(1)}, u32[]{:S(2)}, u32[]{:S(2)}) collective-permute-start(bf16[512,1024]{1,0:T(8,128)(2,1)} %convolution_convert_fusion.21), channel_id=1, source_target_pairs={{0,1},{1,0},{2,3},{3,2},{4,5},{5,4},{6,7},{7,6},{8,9},{9,8},{10,11... | collective-permute-start | bytes 3145736 | tf_op jit(solution)/shard_map/ppermute | solution.py:49
  360.0 46.0 %collective-permute-start.39 = (bf16[512,1024]{1,0:T(8,128)(2,1)S(1)}, bf16[512,1024]{1,0:T(8,128)(2,1)S(1)}, u32[]{:S(2)}, u32[]{:S(2)}) collective-permute-start(bf16[512,1024]{1,0:T(8,128)(2,1)S(1)} %convolution_convert_fusion.19), channel_id=1, source_target_pairs={{0,1},{1,0},{2,3},{3,2},{4,5},{5,4},{6,7},{7,6},{8,9},{9,8},{10,11... | collective-permute-start | bytes 3145736 | tf_op jit(solution)/shard_map/ppermute | solution.py:49
  412.7 49.8 %collective-permute-start.45 = (bf16[512,1024]{1,0:T(8,128)(2,1)}, bf16[512,1024]{1,0:T(8,128)(2,1)S(1)}, u32[]{:S(2)}, u32[]{:S(2)}) collective-permute-start(bf16[512,1024]{1,0:T(8,128)(2,1)} %convolution_convert_fusion.15), channel_id=1, source_target_pairs={{0,1},{1,0},{2,3},{3,2},{4,5},{5,4},{6,7},{7,6},{8,9},{9,8},{10,11... | collective-permute-start | bytes 3145736 | tf_op jit(solution)/shard_map/ppermute | solution.py:49
  450.2 38.8 %collective-permute-start.48 = (bf16[512,1024]{1,0:T(8,128)(2,1)}, bf16[512,1024]{1,0:T(8,128)(2,1)S(1)}, u32[]{:S(2)}, u32[]{:S(2)}) collective-permute-start(bf16[512,1024]{1,0:T(8,128)(2,1)} %fusion.80), channel_id=1, source_target_pairs={{0,1},{1,0},{2,3},{3,2},{4,5},{5,4},{6,7},{7,6},{8,9},{9,8},{10,11... | collective-permute-start | bytes 3145736 | tf_op jit(solution)/shard_map/ppermute | solution.py:49
  463.2 39.0 %collective-permute-start.46 = (bf16[512,1024]{1,0:T(8,128)(2,1)S(1)}, bf16[512,1024]{1,0:T(8,128)(2,1)S(1)}, u32[]{:S(2)}, u32[]{:S(2)}) collective-permute-start(bf16[512,1024]{1,0:T(8,128)(2,1)S(1)} %get-tuple-element.1143), channel_id=1, source_target_pairs={{0,8},{8,0},{16,24},{24,16},{1,9},{9,1},{17,25},{25,17},{2,10},{10... | collective-permute-start | bytes 3145736 | tf_op jit(solution)/shard_map/ppermute | solution.py:282
  491.0 46.4 %collective-permute-start.49 = (bf16[512,1024]{1,0:T(8,128)(2,1)}, bf16[512,1024]{1,0:T(8,128)(2,1)S(1)}, u32[]{:S(2)}, u32[]{:S(2)}) collective-permute-start(bf16[512,1024]{1,0:T(8,128)(2,1)} %get-tuple-element.1183), channel_id=1, source_target_pairs={{0,8},{8,0},{16,24},{24,16},{1,9},{9,1},{17,25},{25,17},{2,10},{10... | collective-permute-start | bytes 3145736 | tf_op jit(solution)/shard_map/ppermute | solution.py:282
  494.7 39.4 %collective-permute-start.51 = (bf16[512,1024]{1,0:T(8,128)(2,1)}, bf16[512,1024]{1,0:T(8,128)(2,1)}, u32[]{:S(2)}, u32[]{:S(2)}) collective-permute-start(bf16[512,1024]{1,0:T(8,128)(2,1)} %fusion.86), channel_id=1, source_target_pairs={{0,1},{1,0},{2,3},{3,2},{4,5},{5,4},{6,7},{7,6},{8,9},{9,8},{10,11... | collective-permute-start | bytes 3145736 | tf_op jit(solution)/shard_map/ppermute | solution.py:49
  546.3 36.3 %collective-permute-start.53 = (bf16[512,1024]{1,0:T(8,128)(2,1)S(1)}, bf16[512,1024]{1,0:T(8,128)(2,1)}, u32[]{:S(2)}, u32[]{:S(2)}) collective-permute-start(bf16[512,1024]{1,0:T(8,128)(2,1)S(1)} %add_convert_fusion.26), channel_id=1, source_target_pairs={{8,16},{16,8},{9,17},{17,9},{10,18},{18,10},{11,19},{19,11},{12,20... | collective-permute-start | bytes 3145736 | tf_op jit(solution)/shard_map/ppermute | solution.py:294
  554.0 54.1 %collective-permute-start.58 = (bf16[512,1024]{1,0:T(8,128)(2,1)}, bf16[512,1024]{1,0:T(8,128)(2,1)}, u32[]{:S(2)}, u32[]{:S(2)}) collective-permute-start(bf16[512,1024]{1,0:T(8,128)(2,1)} %convolution_convert_fusion.11), channel_id=1, source_target_pairs={{0,1},{1,0},{2,3},{3,2},{4,5},{5,4},{6,7},{7,6},{8,9},{9,8},{10,11... | collective-permute-start | bytes 3145736 | tf_op jit(solution)/shard_map/ppermute | solution.py:49
  568.7 35.2 %collective-permute-start.59 = (bf16[512,2048]{1,0:T(8,128)(2,1)}, bf16[512,2048]{1,0:T(8,128)(2,1)}, u32[]{:S(2)}, u32[]{:S(2)}) collective-permute-start(bf16[512,2048]{1,0:T(8,128)(2,1)} %pad_maximum_fusion.25), channel_id=1, source_target_pairs={{0,2},{1,3},{2,0},{3,1},{4,6},{5,7},{6,4},{7,5},{8,10},{9,11},{10,... | collective-permute-start | bytes 6291464 | tf_op jit(solution)/shard_map/ppermute | solution.py:49
  589.0 48.8 %collective-permute-start.55 = (bf16[512,1024]{1,0:T(8,128)(2,1)}, bf16[512,1024]{1,0:T(8,128)(2,1)}, u32[]{:S(2)}, u32[]{:S(2)}) collective-permute-start(bf16[512,1024]{1,0:T(8,128)(2,1)} %convolution_convert_fusion.9), channel_id=1, source_target_pairs={{0,1},{1,0},{2,3},{3,2},{4,5},{5,4},{6,7},{7,6},{8,9},{9,8},{10,11... | collective-permute-start | bytes 3145736 | tf_op jit(solution)/shard_map/ppermute | solution.py:49
  620.9 39.5 %collective-permute-start.64 = (bf16[512,1024]{1,0:T(8,128)(2,1)}, bf16[512,1024]{1,0:T(8,128)(2,1)}, u32[]{:S(2)}, u32[]{:S(2)}) collective-permute-start(bf16[512,1024]{1,0:T(8,128)(2,1)} %convolution_convert_fusion.7), channel_id=1, source_target_pairs={{0,1},{1,0},{2,3},{3,2},{4,5},{5,4},{6,7},{7,6},{8,9},{9,8},{10,11... | collective-permute-start | bytes 3145736 | tf_op jit(solution)/shard_map/ppermute | solution.py:49
  642.7 35.7 %collective-permute-start.74 = (bf16[256,1024]{1,0:T(8,128)(2,1)S(1)}, bf16[256,1024]{1,0:T(8,128)(2,1)S(1)}, u32[]{:S(2)}, u32[]{:S(2)}) collective-permute-start(bf16[256,1024]{1,0:T(8,128)(2,1)S(1)} %get-tuple-element.1563), channel_id=1, source_target_pairs={{1,4},{3,6},{4,1},{6,3},{9,12},{11,14},{12,9},{14,11},{17,20},{19,... | collective-permute-start | bytes 1572872 | tf_op jit(solution)/shard_map/ppermute | solution.py:49
  680.2 40.3 %collective-permute-start.81 = (bf16[512,1024]{1,0:T(8,128)(2,1)S(1)}, bf16[512,1024]{1,0:T(8,128)(2,1)S(1)}, u32[]{:S(2)}, u32[]{:S(2)}) collective-permute-start(bf16[512,1024]{1,0:T(8,128)(2,1)S(1)} %convolution_convert_fusion.3), channel_id=1, source_target_pairs={{0,1},{1,0},{2,3},{3,2},{4,5},{5,4},{6,7},{7,6},{8,9},{9,8},{10,11... | collective-permute-start | bytes 3145736 | tf_op jit(solution)/shard_map/ppermute | solution.py:49
  739.9 48.7 %collective-permute-start.86 = (bf16[512,1024]{1,0:T(8,128)(2,1)S(1)}, bf16[512,1024]{1,0:T(8,128)(2,1)S(1)}, u32[]{:S(2)}, u32[]{:S(2)}) collective-permute-start(bf16[512,1024]{1,0:T(8,128)(2,1)S(1)} %add_convert_fusion.4), channel_id=1, source_target_pairs={{0,8},{8,0},{16,24},{24,16},{1,9},{9,1},{17,25},{25,17},{2,10},{10... | collective-permute-start | bytes 3145736 | tf_op jit(solution)/shard_map/ppermute | solution.py:284
  763.5 42.6 %collective-permute-start.85 = (bf16[512,1024]{1,0:T(8,128)(2,1)S(1)}, bf16[512,1024]{1,0:T(8,128)(2,1)S(1)}, u32[]{:S(2)}, u32[]{:S(2)}) collective-permute-start(bf16[512,1024]{1,0:T(8,128)(2,1)S(1)} %add_convert_fusion.2), channel_id=1, source_target_pairs={{0,8},{8,0},{16,24},{24,16},{1,9},{9,1},{17,25},{25,17},{2,10},{10... | collective-permute-start | bytes 3145736 | tf_op jit(solution)/shard_map/ppermute | solution.py:284
  768.7 57.8 %collective-permute-start.88 = (bf16[512,1024]{1,0:T(8,128)(2,1)S(1)}, bf16[512,1024]{1,0:T(8,128)(2,1)S(1)}, u32[]{:S(2)}, u32[]{:S(2)}) collective-permute-start(bf16[512,1024]{1,0:T(8,128)(2,1)S(1)} %add_convert_fusion.1), channel_id=1, source_target_pairs={{0,8},{8,0},{16,24},{24,16},{1,9},{9,1},{17,25},{25,17},{2,10},{10... | collective-permute-start | bytes 3145736 | tf_op jit(solution)/shard_map/ppermute | solution.py:284
  (161 other events, 2508.0 us)
